TPU v7x, 128 devices: a whole 4x4x4 slice. The times are simulated.
128 devices in a mesh: gx: 4 (over z), gy: 4 (over x), gz: 8 (over y, core).
Axes of the slice: x: 4, y: 4, z: 4, core: 2. Of those that a mesh axis runs over, the one named last changes fastest.
Arguments:
- orbitals: float32 [16, 128, 64, 512], P(None, 'gz', 'gy', 'gx'), may hold values from -12 to 12
- potential: float32 [128, 64, 512], P('gz', 'gy', 'gx'), may hold values from -4 to 4
Outputs:
- orthonormal: float32 [16, 128, 64, 512], P(None, 'gz', 'gy', 'gx')
- factor: float32 [16, 16], replicated
All inputs are finite; a program needn't handle non-finite values.
Results may differ from a plain program's by a relative error of at most 0.00016.
Values sent between devices are 32-bit elements; how exact they have to be, the bound alone decides.
A program may use at most 192 MiB of HBM per device.

v0:
```python
import jax
import jax.numpy as jnp
from jax import lax
from jax.sharding import PartitionSpec as P

COEFFS = (-205.0 / 72.0, 8.0 / 5.0, -1.0 / 5.0, 8.0 / 315.0, -1.0 / 560.0)
KINETIC = -2.0
CENTRE = 23.0
HALF_WIDTH = 20.0


def padded_2(block, sides, width):
    for axis, dim in sides:
        count = lax.axis_size(axis)
        forward = [(i, i + 1) for i in range(count - 1)]
        forward.append((count - 1, 0))
        backward = [(target, source) for source, target in forward]
        low = lax.ppermute(
            lax.slice_in_dim(block, block.shape[dim] - width, None, axis=dim), axis, forward
        )
        high = lax.ppermute(lax.slice_in_dim(block, 0, width, axis=dim), axis, backward)
        block = jnp.concatenate([low, block, high], axis=dim)
    return block


def neighbour(padded, dimension, offset):
    piece = padded
    for other in (1, 2, 3):
        length = padded.shape[other]
        start = 4 + (offset if other == dimension else 0)
        piece = lax.slice_in_dim(piece, start, length - 8 + start, axis=other)
    return piece


def hamilton(padded, potential_part):
    core = neighbour(padded, 1, 0)
    total = 3.0 * COEFFS[0] * core
    for dimension in (1, 2, 3):
        for offset in range(1, 5):
            total = total + COEFFS[offset] * (
                neighbour(padded, dimension, offset) + neighbour(padded, dimension, -offset)
            )
    return KINETIC * total + potential_part * core


def rim_layers(field):
    return padded_2(field, (("gx", 3), ("gy", 2), ("gz", 1)), 4)


def on_device(orbitals, potential):
    level_one = (hamilton(rim_layers(orbitals), potential) - CENTRE * orbitals) / HALF_WIDTH
    level_two = (
        2.0 * (hamilton(rim_layers(level_one), potential) - CENTRE * level_one) / HALF_WIDTH
        - orbitals
    )
    filtered = (
        2.0 * (hamilton(rim_layers(level_two), potential) - CENTRE * level_two) / HALF_WIDTH
        - level_one
    )
    flat = filtered.reshape(filtered.shape[0], -1)
    all_cells = flat.shape[1] * lax.axis_size(("gx", "gy", "gz"))
    local_gram = jnp.einsum("ac,bc->ab", flat, flat, precision=lax.Precision.HIGHEST) / jnp.float32(
        all_cells
    )
    gram = lax.psum(local_gram, ("gx", "gy", "gz"))
    lower = jnp.linalg.cholesky(gram)
    upper = lower.T
    solved = lax.linalg.triangular_solve(lower, flat, left_side=True, lower=True)
    return (solved.reshape(filtered.shape), upper)


def solution(mesh):
    in_specs = (P(None, "gz", "gy", "gx"), P("gz", "gy", "gx"))
    out_specs = (P(None, "gz", "gy", "gx"), P())
    return jax.shard_map(
        on_device, mesh=mesh, in_specs=in_specs, out_specs=out_specs, check_vma=False
    )
```

profile of v0, /device:TPU:1, one launch (start us, length us, event | category | flops | bytes accessed | tf_op | source)
XLA Modules:
  0.0 411.9 jit_solution(15314696078976909693)
XLA Ops:
  0.6 4.2 %fusion.134 = (f32[16,16,16,4]{3,2,1,0:T(8,128)S(1)}, f32[16,16,16,4]{3,2,1,0:T(8,128)}) fusion(f32[16,16,16,128]{3,2,1,0:T(8,128)} %param.2), kind=kLoop, calls=%fused_computation.262 | loop fusion | bytes 262144 | tf_op jit(solution)/shard_map/slice | solution.py:21
  4.8 3.3 copy.142
  17.6 6.8 %collective-permute-done = f32[16,16,16,4]{2,1,3,0:T(8,128)S(1)} collective-permute-done((f32[16,16,16,4]{2,1,3,0:T(8,128)S(1)}, f32[16,16,16,4]{2,1,3,0:T(8,128)S(1)}, u32[]{:S(2)}, u32[]{:S(2)}) %collective-permute-start) | collective-permute-done | bytes 65568 | tf_op jit(solution)/shard_map/ppermute | solution.py:18
  24.4 2.9 copy.93
  27.4 3.9 copy.95
  36.7 21.8 %collective-permute-done.2 = f32[16,16,4,136]{3,1,2,0:T(8,128)S(1)} collective-permute-done((f32[16,16,4,136]{3,1,2,0:T(8,128)S(1)}, f32[16,16,4,136]{3,1,2,0:T(8,128)S(1)}, u32[]{:S(2)}, u32[]{:S(2)}) %collective-permute-start.2) | collective-permute-done | bytes 557088 | tf_op jit(solution)/shard_map/ppermute | solution.py:18
  65.1 5.8 %pad_maximum_fusion = (f32[16,16,20,136]{3,1,2,0:T(8,128)S(1)}, f32[16,16,20,136]{3,1,2,0:T(8,128)}) fusion(f32[16,16,4,136]{3,1,2,0:T(8,128)S(1)} %collective-permute-done.3, f32[16,16,16,4]{3,1,2,0:T(8,128)S(1)} %copy-done.8, f32[16,16,16,128]{3,1,2,0:T(8,128)S(1)} %copy.90, f32[16,16,16,4]{3,1,2,0:T(8,128)S(1)} %copy-done.5, ...), kind=kLoop, calls=%fused_computation.36 | loop fusion | flops 4177920 | bytes 8912896 | tf_op jit(solution)/shard_map/concatenate | solution.py:22
  70.9 12.2 %collective-permute-done.4 = f32[16,4,24,136]{3,2,1,0:T(8,128)S(1)} collective-permute-done((f32[16,4,24,136]{3,2,1,0:T(8,128)S(1)}, f32[16,4,24,136]{3,2,1,0:T(8,128)S(1)}, u32[]{:S(2)}, u32[]{:S(2)}) %collective-permute-start.4) | collective-permute-done | bytes 835616 | tf_op jit(solution)/shard_map/ppermute | solution.py:21
  86.8 24.3 %broadcast_multiply_fusion = (f32[16,16,16,128]{3,1,2,0:T(8,128)S(1)}, f32[16,16,16,128]{3,1,2,0:T(8,128)}) fusion(f32[16,16,16,128]{3,1,2,0:T(8,128)S(1)} %copy-done.3, f32[16,16,128]{2,0,1:T(8,128)S(1)} %copy.104, f32[16,16,16,4]{3,1,2,0:T(8,128)S(1)} %copy-done.5, f32[16,16,16,4]{3,1,2,0:T(8,128)S(1)} %copy-done.8, ...), kind=kLoop, calls=%fused_computation.248 | loop fusion | flops 47710208 | bytes 26116096 | tf_op jit(solution)/shard_map/div | solution.py:51
  111.0 2.7 fusion.133
  113.7 3.3 copy.107
  117.4 4.1 copy.108
  123.9 7.1 %collective-permute-done.6 = f32[16,16,16,4]{2,1,3,0:T(8,128)S(1)} collective-permute-done((f32[16,16,16,4]{2,1,3,0:T(8,128)S(1)}, f32[16,16,16,4]{2,1,3,0:T(8,128)S(1)}, u32[]{:S(2)}, u32[]{:S(2)}) %collective-permute-start.6) | collective-permute-done | bytes 65568 | tf_op jit(solution)/shard_map/ppermute | solution.py:18
  131.0 2.9 copy.109
  134.9 3.9 copy.110
  144.7 21.4 %collective-permute-done.8 = f32[16,16,4,136]{3,1,2,0:T(8,128)S(1)} collective-permute-done((f32[16,16,4,136]{3,1,2,0:T(8,128)S(1)}, f32[16,16,4,136]{3,1,2,0:T(8,128)S(1)}, u32[]{:S(2)}, u32[]{:S(2)}) %collective-permute-start.8) | collective-permute-done | bytes 557088 | tf_op jit(solution)/shard_map/ppermute | solution.py:18
  168.8 2.6 collective-permute-start.10
  173.4 5.8 %pad_maximum_fusion.1 = (f32[16,16,20,136]{3,1,2,0:T(8,128)S(1)}, f32[16,16,20,136]{3,1,2,0:T(8,128)}) fusion(f32[16,16,4,136]{3,1,2,0:T(8,128)S(1)} %collective-permute-done.9, f32[16,16,16,4]{3,1,2,0:T(8,128)S(1)} %copy-done.7, f32[16,16,16,128]{3,1,2,0:T(8,128)S(1)} %get-tuple-element.12, f32[16,16,16,4]{3,1,2,0:T(8,128)S(1)} %copy-done.4, ...), kind=kLoop, calls=%fused_computation.38 | loop fusion | flops 4177920 | bytes 8912896 | tf_op jit(solution)/shard_map/concatenate | solution.py:22
  179.1 12.2 %collective-permute-done.10 = f32[16,4,24,136]{3,2,1,0:T(8,128)S(1)} collective-permute-done((f32[16,4,24,136]{3,2,1,0:T(8,128)S(1)}, f32[16,4,24,136]{3,2,1,0:T(8,128)S(1)}, u32[]{:S(2)}, u32[]{:S(2)}) %collective-permute-start.10) | collective-permute-done | bytes 835616 | tf_op jit(solution)/shard_map/ppermute | solution.py:21
  195.0 23.8 %fusion.30 = f32[16,16,16,128]{3,1,2,0:T(8,128)S(1)} fusion(f32[16,16,16,4]{3,1,2,0:T(8,128)S(1)} %copy-done.4, f32[16,16,16,128]{3,1,2,0:T(8,128)S(1)} %get-tuple-element.12, f32[16,16,16,4]{3,1,2,0:T(8,128)S(1)} %copy-done.7, f32[16,16,20,136]{3,1,2,0:T(8,128)} %get-tuple-element.25, f32[16,16,20,136]{3,1,2,0:T(8,128)S(1)} %get-tuple-element.24, ...), kind=kLoop, calls=%fused_computation.72 | loop fusion | flops 48234496 | bytes 28213248 | tf_op jit(solution)/shard_map/sub | solution.py:53
  220.9 3.3 copy.119
  230.1 8.7 %collective-permute-done.12 = f32[16,16,16,4]{2,1,3,0:T(8,128)S(1)} collective-permute-done((f32[16,16,16,4]{2,1,3,0:T(8,128)S(1)}, f32[16,16,16,4]{2,1,3,0:T(8,128)S(1)}, u32[]{:S(2)}, u32[]{:S(2)}) %collective-permute-start.12) | collective-permute-done | bytes 65568 | tf_op jit(solution)/shard_map/ppermute | solution.py:18
  238.8 2.9 copy.121
  241.7 4.0 copy.122
  245.7 2.6 pad_maximum_fusion.54
  251.2 21.8 %collective-permute-done.14 = f32[16,16,4,136]{3,1,2,0:T(8,128)S(1)} collective-permute-done((f32[16,16,4,136]{3,1,2,0:T(8,128)S(1)}, f32[16,16,4,136]{3,1,2,0:T(8,128)S(1)}, u32[]{:S(2)}, u32[]{:S(2)}) %collective-permute-start.14) | collective-permute-done | bytes 557088 | tf_op jit(solution)/shard_map/ppermute | solution.py:18
  279.1 5.8 %pad_maximum_fusion.2 = (f32[16,16,20,136]{3,1,2,0:T(8,128)S(1)}, f32[16,16,20,136]{3,1,2,0:T(8,128)}) fusion(f32[16,16,4,136]{3,1,2,0:T(8,128)S(1)} %collective-permute-done.15, f32[16,16,16,4]{3,1,2,0:T(8,128)S(1)} %copy-done.9, f32[16,16,16,128]{3,1,2,0:T(8,128)S(1)} %copy-done.1, f32[16,16,16,4]{3,1,2,0:T(8,128)S(1)} %copy-done.6, ...), kind=kLoop, calls=%fused_computation.40 | loop fusion | flops 4177920 | bytes 8912896 | tf_op jit(solution)/shard_map/concatenate | solution.py:22
  284.8 12.3 %collective-permute-done.16 = f32[16,4,24,136]{3,2,1,0:T(8,128)S(1)} collective-permute-done((f32[16,4,24,136]{3,2,1,0:T(8,128)S(1)}, f32[16,4,24,136]{3,2,1,0:T(8,128)S(1)}, u32[]{:S(2)}, u32[]{:S(2)}) %collective-permute-start.16) | collective-permute-done | bytes 835616 | tf_op jit(solution)/shard_map/ppermute | solution.py:21
  300.8 24.5 %fusion.9 = f32[16,16,16,128]{3,1,2,0:T(8,128)} fusion(f32[16,16,16,4]{3,1,2,0:T(8,128)S(1)} %copy-done.6, f32[16,16,16,128]{3,1,2,0:T(8,128)S(1)} %copy-done.1, f32[16,16,16,4]{3,1,2,0:T(8,128)S(1)} %copy-done.9, f32[16,16,20,136]{3,1,2,0:T(8,128)} %get-tuple-element.21, f32[16,16,20,136]{3,1,2,0:T(8,128)S(1)} %get-tuple-element.20, ...), kind=kLoop, calls=%fused_computation.51 | loop fusion | flops 48758784 | bytes 26116096 | tf_op jit(solution)/shard_map/sub | solution.py:57
  325.4 6.9 %fusion.125 = f32[16,16]{0,1:T(8,128)S(1)} fusion(f32[16,16,16,128]{3,1,2,0:T(8,128)} %fusion.9), kind=kOutput, calls=%fused_computation.238 | convolution fusion | flops 100663552 | bytes 2098176 | tf_op jit(solution)/shard_map/ac,bc->ab/dot_general | solution.py:62
  333.0 67.5 %psum.7 = f32[16,16]{0,1:T(8,128)S(1)} all-reduce(f32[16,16]{0,1:T(8,128)S(1)} %fusion.125), channel_id=1, replica_groups=mesh['gx'=4,'gy'=4,'gz'=8] {'gx','gy','gz'}, use_global_device_ids=true, to_apply=%region_0.0 | all-reduce | flops 256 | bytes 2048 | tf_op jit(solution)/shard_map/psum | solution.py:65
  406.2 2.9 fusion.118
  (88 shorter events, 72.6 us)
Async XLA Ops:
  8.1 16.3 %collective-permute-start = (f32[16,16,16,4]{2,1,3,0:T(8,128)S(1)}, f32[16,16,16,4]{2,1,3,0:T(8,128)S(1)}, u32[]{:S(2)}, u32[]{:S(2)}) collective-permute-start(f32[16,16,16,4]{2,1,3,0:T(8,128)S(1)} %copy.142), channel_id=1, source_target_pairs={{0,32},{32,64},{64,96},{96,0},{1,33},{33,65},{65,97},{97,1},{2,34}... | collective-permute-start | bytes 196616 | tf_op jit(solution)/shard_map/ppermute | solution.py:18
  13.2 14.1 %collective-permute-start.1 = (f32[16,16,16,4]{2,1,3,0:T(8,128)}, f32[16,16,16,4]{2,1,3,0:T(8,128)}, u32[]{:S(2)}, u32[]{:S(2)}) collective-permute-start(f32[16,16,16,4]{2,1,3,0:T(8,128)} %copy.143), channel_id=1, source_target_pairs={{32,0},{64,32},{96,64},{0,96},{33,1},{65,33},{97,65},{1,97},{34,2}... | collective-permute-start | bytes 196616 | tf_op jit(solution)/shard_map/ppermute | solution.py:21
  17.6 47.5 %copy-start.2 = (f32[16,16,16,128]{3,1,2,0:T(8,128)}, f32[16,16,16,128]{3,1,2,0:T(8,128)S(1)}, u32[]{:S(2)}) copy-start(f32[16,16,16,128]{3,1,2,0:T(8,128)S(1)} %copy.90) | copy-start | bytes 6291460
  31.3 27.3 %copy-start.5 = (f32[16,16,16,4]{3,1,2,0:T(8,128)S(1)}, f32[16,16,16,4]{3,1,2,0:T(8,128)}, u32[]{:S(2)}) copy-start(f32[16,16,16,4]{3,1,2,0:T(8,128)} %copy.93) | copy-start | bytes 196612
  31.3 27.3 %copy-start.8 = (f32[16,16,16,4]{3,1,2,0:T(8,128)S(1)}, f32[16,16,16,4]{3,1,2,0:T(8,128)}, u32[]{:S(2)}) copy-start(f32[16,16,16,4]{3,1,2,0:T(8,128)} %copy.95) | copy-start | bytes 196612
  33.8 24.7 %collective-permute-start.2 = (f32[16,16,4,136]{3,1,2,0:T(8,128)S(1)}, f32[16,16,4,136]{3,1,2,0:T(8,128)S(1)}, u32[]{:S(2)}, u32[]{:S(2)}) collective-permute-start(f32[16,16,4,136]{3,1,2,0:T(8,128)S(1)} %get-tuple-element.31), channel_id=1, source_target_pairs={{0,8},{8,16},{16,24},{24,0},{1,9},{9,17},{17,25},{25,1},{2,10},{10... | collective-permute-start | bytes 1671176 | tf_op jit(solution)/shard_map/ppermute | solution.py:18
  35.1 23.4 %collective-permute-start.3 = (f32[16,16,4,136]{3,1,2,0:T(8,128)S(1)}, f32[16,16,4,136]{3,1,2,0:T(8,128)S(1)}, u32[]{:S(2)}, u32[]{:S(2)}) collective-permute-start(f32[16,16,4,136]{3,1,2,0:T(8,128)S(1)} %get-tuple-element.30), channel_id=1, source_target_pairs={{8,0},{16,8},{24,16},{0,24},{9,1},{17,9},{25,17},{1,25},{10,2},{18... | collective-permute-start | bytes 1671176 | tf_op jit(solution)/shard_map/ppermute | solution.py:21
  61.2 3.8 copy-start.12
  61.2 21.9 %collective-permute-start.4 = (f32[16,4,24,136]{3,2,1,0:T(8,128)S(1)}, f32[16,4,24,136]{3,2,1,0:T(8,128)S(1)}, u32[]{:S(2)}, u32[]{:S(2)}) collective-permute-start(f32[16,4,24,136]{3,2,1,0:T(8,128)S(1)} %copy.96), channel_id=1, source_target_pairs={{1,0},{2,1},{3,2},{4,3},{5,4},{6,5},{7,6},{0,7},{9,8},{10,9},{11,1... | collective-permute-start | bytes 2506760 | tf_op jit(solution)/shard_map/ppermute | solution.py:21
  63.8 21.2 %collective-permute-start.5 = (f32[16,4,24,136]{3,2,1,0:T(8,128)S(1)}, f32[16,4,24,136]{3,2,1,0:T(8,128)S(1)}, u32[]{:S(2)}, u32[]{:S(2)}) collective-permute-start(f32[16,4,24,136]{3,2,1,0:T(8,128)S(1)} %copy.98), channel_id=1, source_target_pairs={{0,1},{1,2},{2,3},{3,4},{4,5},{5,6},{6,7},{7,0},{8,9},{9,10},{10,1... | collective-permute-start | bytes 2506760 | tf_op jit(solution)/shard_map/ppermute | solution.py:18
  85.0 1.8 copy-start.3
  117.0 14.0 %collective-permute-start.6 = (f32[16,16,16,4]{2,1,3,0:T(8,128)S(1)}, f32[16,16,16,4]{2,1,3,0:T(8,128)S(1)}, u32[]{:S(2)}, u32[]{:S(2)}) collective-permute-start(f32[16,16,16,4]{2,1,3,0:T(8,128)S(1)} %copy.107), channel_id=1, source_target_pairs={{0,32},{32,64},{64,96},{96,0},{1,33},{33,65},{65,97},{97,1},{2,34}... | collective-permute-start | bytes 196616 | tf_op jit(solution)/shard_map/ppermute | solution.py:18
  121.5 13.4 %collective-permute-start.7 = (f32[16,16,16,4]{2,1,3,0:T(8,128)}, f32[16,16,16,4]{2,1,3,0:T(8,128)}, u32[]{:S(2)}, u32[]{:S(2)}) collective-permute-start(f32[16,16,16,4]{2,1,3,0:T(8,128)} %copy.108), channel_id=1, source_target_pairs={{32,0},{64,32},{96,64},{0,96},{33,1},{65,33},{97,65},{1,97},{34,2}... | collective-permute-start | bytes 196616 | tf_op jit(solution)/shard_map/ppermute | solution.py:21
  138.8 27.4 %copy-start.4 = (f32[16,16,16,4]{3,1,2,0:T(8,128)S(1)}, f32[16,16,16,4]{3,1,2,0:T(8,128)}, u32[]{:S(2)}) copy-start(f32[16,16,16,4]{3,1,2,0:T(8,128)} %copy.109) | copy-start | bytes 196612
  138.8 27.4 %copy-start.7 = (f32[16,16,16,4]{3,1,2,0:T(8,128)S(1)}, f32[16,16,16,4]{3,1,2,0:T(8,128)}, u32[]{:S(2)}) copy-start(f32[16,16,16,4]{3,1,2,0:T(8,128)} %copy.110) | copy-start | bytes 196612
  141.4 24.7 %collective-permute-start.8 = (f32[16,16,4,136]{3,1,2,0:T(8,128)S(1)}, f32[16,16,4,136]{3,1,2,0:T(8,128)S(1)}, u32[]{:S(2)}, u32[]{:S(2)}) collective-permute-start(f32[16,16,4,136]{3,1,2,0:T(8,128)S(1)} %get-tuple-element.27), channel_id=1, source_target_pairs={{0,8},{8,16},{16,24},{24,0},{1,9},{9,17},{17,25},{25,1},{2,10},{10... | collective-permute-start | bytes 1671176 | tf_op jit(solution)/shard_map/ppermute | solution.py:18
  142.8 23.4 %collective-permute-start.9 = (f32[16,16,4,136]{3,1,2,0:T(8,128)S(1)}, f32[16,16,4,136]{3,1,2,0:T(8,128)S(1)}, u32[]{:S(2)}, u32[]{:S(2)}) collective-permute-start(f32[16,16,4,136]{3,1,2,0:T(8,128)S(1)} %get-tuple-element.26), channel_id=1, source_target_pairs={{8,0},{16,8},{24,16},{0,24},{9,1},{17,9},{25,17},{1,25},{10,2},{18... | collective-permute-start | bytes 1671176 | tf_op jit(solution)/shard_map/ppermute | solution.py:21
  168.8 22.6 %collective-permute-start.10 = (f32[16,4,24,136]{3,2,1,0:T(8,128)S(1)}, f32[16,4,24,136]{3,2,1,0:T(8,128)S(1)}, u32[]{:S(2)}, u32[]{:S(2)}) collective-permute-start(f32[16,4,24,136]{3,2,1,0:T(8,128)S(1)} %copy.111), channel_id=1, source_target_pairs={{1,0},{2,1},{3,2},{4,3},{5,4},{6,5},{7,6},{0,7},{9,8},{10,9},{11,1... | collective-permute-start | bytes 2506760 | tf_op jit(solution)/shard_map/ppermute | solution.py:21
  171.7 21.6 %collective-permute-start.11 = (f32[16,4,24,136]{3,2,1,0:T(8,128)S(1)}, f32[16,4,24,136]{3,2,1,0:T(8,128)S(1)}, u32[]{:S(2)}, u32[]{:S(2)}) collective-permute-start(f32[16,4,24,136]{3,2,1,0:T(8,128)S(1)} %copy.113), channel_id=1, source_target_pairs={{0,1},{1,2},{2,3},{3,4},{4,5},{5,6},{6,7},{7,0},{8,9},{9,10},{10,1... | collective-permute-start | bytes 2506760 | tf_op jit(solution)/shard_map/ppermute | solution.py:18
  218.9 2.1 copy-start
  224.2 14.6 %collective-permute-start.12 = (f32[16,16,16,4]{2,1,3,0:T(8,128)S(1)}, f32[16,16,16,4]{2,1,3,0:T(8,128)S(1)}, u32[]{:S(2)}, u32[]{:S(2)}) collective-permute-start(f32[16,16,16,4]{2,1,3,0:T(8,128)S(1)} %copy.119), channel_id=1, source_target_pairs={{0,32},{32,64},{64,96},{96,0},{1,33},{33,65},{65,97},{97,1},{2,34}... | collective-permute-start | bytes 196616 | tf_op jit(solution)/shard_map/ppermute | solution.py:18
  227.7 17.9 %copy-start.1 = (f32[16,16,16,128]{3,1,2,0:T(8,128)S(1)}, f32[16,16,16,128]{3,1,2,0:T(8,128)}, u32[]{:S(2)}) copy-start(f32[16,16,16,128]{3,1,2,0:T(8,128)} %copy-done) | copy-start | bytes 6291460
  227.7 14.0 %collective-permute-start.13 = (f32[16,16,16,4]{2,1,3,0:T(8,128)}, f32[16,16,16,4]{2,1,3,0:T(8,128)}, u32[]{:S(2)}, u32[]{:S(2)}) collective-permute-start(f32[16,16,16,4]{2,1,3,0:T(8,128)} %copy.120), channel_id=1, source_target_pairs={{32,0},{64,32},{96,64},{0,96},{33,1},{65,33},{97,65},{1,97},{34,2}... | collective-permute-start | bytes 196616 | tf_op jit(solution)/shard_map/ppermute | solution.py:21
  245.7 27.4 %copy-start.6 = (f32[16,16,16,4]{3,1,2,0:T(8,128)S(1)}, f32[16,16,16,4]{3,1,2,0:T(8,128)}, u32[]{:S(2)}) copy-start(f32[16,16,16,4]{3,1,2,0:T(8,128)} %copy.121) | copy-start | bytes 196612
  245.7 27.4 %copy-start.9 = (f32[16,16,16,4]{3,1,2,0:T(8,128)S(1)}, f32[16,16,16,4]{3,1,2,0:T(8,128)}, u32[]{:S(2)}) copy-start(f32[16,16,16,4]{3,1,2,0:T(8,128)} %copy.122) | copy-start | bytes 196612
  248.2 24.8 %collective-permute-start.14 = (f32[16,16,4,136]{3,1,2,0:T(8,128)S(1)}, f32[16,16,4,136]{3,1,2,0:T(8,128)S(1)}, u32[]{:S(2)}, u32[]{:S(2)}) collective-permute-start(f32[16,16,4,136]{3,1,2,0:T(8,128)S(1)} %get-tuple-element.23), channel_id=1, source_target_pairs={{0,8},{8,16},{16,24},{24,0},{1,9},{9,17},{17,25},{25,1},{2,10},{10... | collective-permute-start | bytes 1671176 | tf_op jit(solution)/shard_map/ppermute | solution.py:18
  249.5 23.6 %collective-permute-start.15 = (f32[16,16,4,136]{3,1,2,0:T(8,128)S(1)}, f32[16,16,4,136]{3,1,2,0:T(8,128)S(1)}, u32[]{:S(2)}, u32[]{:S(2)}) collective-permute-start(f32[16,16,4,136]{3,1,2,0:T(8,128)S(1)} %get-tuple-element.22), channel_id=1, source_target_pairs={{8,0},{16,8},{24,16},{0,24},{9,1},{17,9},{25,17},{1,25},{10,2},{18... | collective-permute-start | bytes 1671176 | tf_op jit(solution)/shard_map/ppermute | solution.py:21
  275.7 21.5 %collective-permute-start.16 = (f32[16,4,24,136]{3,2,1,0:T(8,128)S(1)}, f32[16,4,24,136]{3,2,1,0:T(8,128)S(1)}, u32[]{:S(2)}, u32[]{:S(2)}) collective-permute-start(f32[16,4,24,136]{3,2,1,0:T(8,128)S(1)} %copy.123), channel_id=1, source_target_pairs={{1,0},{2,1},{3,2},{4,3},{5,4},{6,5},{7,6},{0,7},{9,8},{10,9},{11,1... | collective-permute-start | bytes 2506760 | tf_op jit(solution)/shard_map/ppermute | solution.py:21
  278.2 20.8 %collective-permute-start.17 = (f32[16,4,24,136]{3,2,1,0:T(8,128)S(1)}, f32[16,4,24,136]{3,2,1,0:T(8,128)S(1)}, u32[]{:S(2)}, u32[]{:S(2)}) collective-permute-start(f32[16,4,24,136]{3,2,1,0:T(8,128)S(1)} %copy.125), channel_id=1, source_target_pairs={{0,1},{1,2},{2,3},{3,4},{4,5},{5,6},{6,7},{7,0},{8,9},{9,10},{10,1... | collective-permute-start | bytes 2506760 | tf_op jit(solution)/shard_map/ppermute | solution.py:18
  299.0 1.8 copy-start.10
  325.4 6.9 %copy-start.11 = (f32[16,16,16,128]{3,1,2,0:T(8,128)S(1)}, f32[16,16,16,128]{3,1,2,0:T(8,128)}, u32[]{:S(2)}) copy-start(f32[16,16,16,128]{3,1,2,0:T(8,128)} %fusion.9) | copy-start | bytes 6291460
where the time goes:
time: 418 us; the launch traced here: 412 us
  waiting for transfers between devices  125 us (30%)
  other arithmetic  109 us (26%)
  local copies, waits for them, and re-layouts  68.6 us (16%)
  blocking collectives  67.5 us (16%)
  starting transfers between devices  30.8 us (7%)
  matrix products  9.79 us (2%)
    ppermute x9, waiting for transfers between devices, padded_2(): lax.ppermute(lax.slice_in_dim(block, block.shape[dim] - width, None, axis...  87.6 us
    psum x1, blocking collectives, on_device(): gram = lax.psum(local_gram, ('gx', 'gy', 'gz'))  67.5 us
    ppermute x9, waiting for transfers between devices, padded_2(): lax.ppermute(lax.slice_in_dim(block, 0, width, axis=dim), axis, backward)  37.8 us
    concatenate x6, other arithmetic, padded_2(): block = jnp.concatenate([low, block, high], axis=dim)  25 us
    sub x1, other arithmetic, on_device(): 2.0 * (hamilton(rim_layers(level_two), potential) - CENTRE * level_two)  24.5 us
    div x1, other arithmetic, on_device(): (hamilton(rim_layers(orbitals), potential) - CENTRE * orbitals) / HALF_WIDTH  24.3 us
    sub x1, other arithmetic, on_device(): 2.0 * (hamilton(rim_layers(level_one), potential) - CENTRE * level_one)  23.8 us
    ppermute x9, starting transfers between devices, padded_2(): lax.ppermute(lax.slice_in_dim(block, 0, width, axis=dim), axis, backward)  19.4 us
  transfers between devices with their start and end apart: 18, of which 11 were waited for; matrix products, arithmetic and copies ran while one was open for 11% of the time, Pallas kernels for 0%

commit v1 on v0

v1 whole, which is shorter than its diff:
```python
import functools

import jax
import jax.numpy as jnp
import ml_dtypes
import numpy as np
from jax import lax
from jax.experimental import pallas as pl
from jax.experimental.pallas import tpu as pltpu
from jax.sharding import PartitionSpec as P

COEFFS = (-205.0 / 72.0, 8.0 / 5.0, -1.0 / 5.0, 8.0 / 315.0, -1.0 / 560.0)
SCALE = 2.0 * -2.0 / 20.0
TAPS = tuple(SCALE * c for c in COEFFS)

NORB, LZ, LY, LX = 16, 16, 16, 128
HALO = 4
SUB = 8
GROUPS = NORB // SUB
SLABS = 4
CHUNKS = LZ // SLABS
UNITS = GROUPS * CHUNKS
ROWS = LZ * LY
CELLS = 4194304
F32, BF16 = jnp.float32, jnp.bfloat16
MESH = pl.DeviceIdType.MESH
AXES = ("gx", "gy", "gz")


def x_weights():
    places = np.concatenate([np.arange(LX), np.arange(-HALO, 0), np.arange(LX, LX + HALO)])
    away = np.abs(places[:, None] - np.arange(LX)[None, :])
    full = np.zeros((2 * LX, LX), np.float32)
    for k in range(1, HALO + 1):
        full[: len(places)][away == k] = np.float32(TAPS[k])
    high = full.astype(ml_dtypes.bfloat16)
    low = (full - high.astype(np.float32)).astype(ml_dtypes.bfloat16)
    return np.concatenate([high, low], axis=1)


def split(value):
    high = value.astype(BF16)
    return high, (value - high.astype(F32)).astype(BF16)


def filter_kernel(
    orb_hbm, pot_hbm, w_hbm, last, gram_ref,
    load, buf, pack, from_left, from_right, pv, w_ref, part, seen_xy, seen_z,
    load_sem, small_sem, ysend, yrecv, xsend, xrecv, zsend, zrecv, gsend, grecv,
):
    sizes = {axis: lax.axis_size(axis) for axis in AXES}
    here = {axis: lax.axis_index(axis) for axis in AXES}

    def at(axis, step):
        return {axis: lax.rem(here[axis] + (step + sizes[axis]), sizes[axis])}

    def load_copy(g, c):
        part = (pl.ds(g * SUB, SUB), pl.ds(c * SLABS * LY, SLABS * LY))
        return pltpu.make_async_copy(
            orb_hbm.at[part], load.at[part], load_sem.at[g * CHUNKS + c]
        )

    small = [
        pltpu.make_async_copy(pot_hbm, pv, small_sem.at[0]),
        pltpu.make_async_copy(w_hbm, w_ref, small_sem.at[1]),
    ]
    for g in range(GROUPS):
        for c in range(CHUNKS):
            load_copy(g, c).start()
    for copy in small:
        copy.start()

    def in_plane(k):
        other = lax.rem(here["gx"] * sizes["gy"] + here["gy"] + k, sizes["gx"] * sizes["gy"])
        return {"gx": other // sizes["gy"], "gy": lax.rem(other, sizes["gy"])}

    def in_column(k):
        return at("gz", k)

    others = [in_plane(k) for k in range(1, sizes["gx"] * sizes["gy"])]
    others += [in_column(k) for k in range(1, sizes["gz"])]
    barrier = pltpu.get_barrier_semaphore()
    for device in others:
        pl.semaphore_signal(barrier, inc=1, device_id=device, device_id_type=MESH)

    def remote(src, dst, send_sem, recv_sem, axis, step):
        return pltpu.make_async_remote_copy(
            src_ref=src, dst_ref=dst, send_sem=send_sem, recv_sem=recv_sem,
            device_id=at(axis, step), device_id_type=MESH,
        )

    def y_copies(level, g, c):
        u, zs = g * CHUNKS + c, pl.ds(HALO + c * SLABS, SLABS)
        level_buf = buf.at[level, g, zs]
        return [
            remote(
                level_buf.at[:, pl.ds(LY, HALO)], level_buf.at[:, pl.ds(0, HALO)],
                ysend.at[level, u, 0], yrecv.at[level, u, 0], "gy", 1,
            ),
            remote(
                level_buf.at[:, pl.ds(HALO, HALO)], level_buf.at[:, pl.ds(HALO + LY, HALO)],
                ysend.at[level, u, 1], yrecv.at[level, u, 1], "gy", -1,
            ),
        ]

    def x_copies(level, g, c):
        u, zs = g * CHUNKS + c, pl.ds(c * SLABS, SLABS)
        return [
            remote(
                pack.at[level, g, zs], from_left.at[level, g, zs],
                xsend.at[level, u, 0], xrecv.at[level, u, 0], "gx", 1,
            ),
            remote(
                pack.at[level, g, zs], from_right.at[level, g, zs],
                xsend.at[level, u, 1], xrecv.at[level, u, 1], "gx", -1,
            ),
        ]

    def z_copy(level, g, up):
        inner = pl.ds(HALO, LY)
        src, dst = (LZ, 0) if up else (HALO, HALO + LZ)
        i = 0 if up else 1
        return remote(
            buf.at[level, g, pl.ds(src, HALO), inner], buf.at[level, g, pl.ds(dst, HALO), inner],
            zsend.at[level, g, i], zrecv.at[level, g, i], "gz", 1 if up else -1,
        )

    def send(level, g, c):
        for copy in y_copies(level, g, c):
            copy.start()

        @pl.when(c == 0)
        def _():
            z_copy(level, g, False).start()

        @pl.when(c == CHUNKS - 1)
        def _():
            z_copy(level, g, True).start()

        for copy in x_copies(level, g, c):
            copy.start()

    lane = lax.broadcasted_iota(jnp.int32, (SUB, LX), 1)

    def pack_edges(values):
        packed = jnp.zeros((SUB, LX), F32)
        for y in range(LY):
            moved = pltpu.roll(values[y], 2 * HALO * y + HALO, 1)
            mine = (lane >= 2 * HALO * y) & (lane < 2 * HALO * (y + 1))
            packed = jnp.where(mine, moved, packed)
        return packed

    flat = load.reshape(NORB * ROWS, LX)

    def start_unit(g, c):
        load_copy(g, c).wait()

        @pl.loop(0, SLABS)
        def _(s):
            z = c * SLABS + s
            values = []
            for y in range(LY):
                v = flat[pl.ds(g * SUB * ROWS + z * LY + y, SUB, stride=ROWS), :]
                buf[0, g, HALO + z, HALO + y] = v
                values.append(v)
            pack[0, g, z] = pack_edges(values)

    start_unit(0, 0)
    pl.semaphore_wait(barrier, len(others))
    send(0, 0, 0)

    @pl.loop(1, UNITS)
    def _(u):
        g, c = u // CHUNKS, lax.rem(u, CHUNKS)
        start_unit(g, c)
        send(0, g, c)

    for copy in small:
        copy.wait()
    pv[...] = pv[...] * F32(0.1) + F32(3.0 * TAPS[0] - 2.3)

    def stencil(level, g, z):
        w = w_ref[...]
        edges = jnp.where(
            lax.rem(lane, 2 * HALO) < HALO, from_left[level, g, z], from_right[level, g, z]
        )
        centre = [buf[level, g, HALO + z, HALO + y] for y in range(LY)]
        rows = jnp.concatenate(centre, axis=0)
        halo = jnp.concatenate(
            [pltpu.roll(edges, (LX - 2 * HALO * y) % LX, 1) for y in range(LY)], axis=0
        )
        high, low = split(jnp.concatenate([rows, halo], axis=1))
        both = jnp.dot(high, w, preferred_element_type=F32)
        along_x = (
            jnp.dot(low, w[:, :LX], preferred_element_type=F32) + both[:, :LX] + both[:, LX:]
        )
        out = []
        for y in range(LY):
            here_v = centre[y]
            total = pv[z, pl.ds(y, 1), :] * here_v + along_x[y * SUB : (y + 1) * SUB]
            for k in range(1, HALO + 1):
                around = (
                    buf[level, g, HALO + z + k, HALO + y] + buf[level, g, HALO + z - k, HALO + y]
                ) + (buf[level, g, HALO + z, HALO + y + k] + buf[level, g, HALO + z, HALO + y - k])
                total = total + F32(TAPS[k]) * around
            out.append(total)
        return out

    def wait_halos(level, g, c):
        for copy in y_copies(level, g, c) + x_copies(level, g, c):
            copy.wait_recv()

        @pl.when(c == 0)
        def _():
            z_copy(level, g, True).wait_recv()

        @pl.when(c == CHUNKS - 1)
        def _():
            z_copy(level, g, False).wait_recv()

    for level in (1, 2):

        @pl.loop(0, UNITS)
        def _(u, level=level):
            g, c = u // CHUNKS, lax.rem(u, CHUNKS)
            wait_halos(level - 1, g, c)

            @pl.loop(0, SLABS)
            def _(s):
                z = c * SLABS + s
                new = stencil(level - 1, g, z)
                if level == 1:
                    new = [F32(0.5) * v for v in new]
                else:
                    new = [v - buf[0, g, HALO + z, HALO + y] for y, v in enumerate(new)]
                for y in range(LY):
                    buf[level, g, HALO + z, HALO + y] = new[y]
                pack[level, g, z] = pack_edges(new)

            send(level, g, c)

    part[...] = jnp.zeros_like(part)

    @pl.loop(0, UNITS)
    def _(u):
        g, c = u // CHUNKS, lax.rem(u, CHUNKS)
        wait_halos(2, g, c)

        @pl.loop(0, SLABS)
        def _(s):
            z = c * SLABS + s
            new = stencil(2, g, z)
            for y in range(LY):
                last[g, z, y] = new[y] - buf[1, g, HALO + z, HALO + y]

        @pl.when(g == GROUPS - 1)
        def _():
            @pl.loop(0, SLABS)
            def _(s):
                z = c * SLABS + s
                wide = jnp.concatenate(
                    [
                        jnp.concatenate([last[k, z, y] for k in range(GROUPS)], axis=0)
                        for y in range(LY)
                    ],
                    axis=1,
                )
                high, low = split(wide)
                both = jnp.concatenate([high, low], axis=0)
                quad = lax.dot_general(
                    both, both, (((1,), (1,)), ((), ())), preferred_element_type=F32
                )
                four = quad[:NORB] + quad[NORB:]
                part[:, :NORB] += four[:, :NORB] + four[:, NORB:]

    gram_copies = []
    moved = pltpu.roll(part[...] * F32(1.0 / CELLS), 0, 1, stride=NORB, stride_axis=0)
    value = jnp.sum(moved.reshape(2, SUB, LX), axis=1)
    plane = sizes["gx"] * sizes["gy"]
    base = 0
    for seen, count, mine, target in (
        (seen_xy, plane, here["gx"] * sizes["gy"] + here["gy"], in_plane),
        (seen_z, sizes["gz"], here["gz"], in_column),
    ):
        seen[mine] = value
        copies = []
        for k in range(1, count):
            copies.append(
                pltpu.make_async_remote_copy(
                    src_ref=seen.at[mine], dst_ref=seen.at[mine], send_sem=gsend.at[base + k - 1],
                    recv_sem=grecv.at[base + k - 1], device_id=target(k), device_id_type=MESH,
                )
            )
            copies[-1].start()
        for k in range(1, count):
            came_from = lax.rem(mine + count - k, count)
            pltpu.make_async_remote_copy(
                src_ref=seen.at[came_from], dst_ref=seen.at[came_from],
                send_sem=gsend.at[base + k - 1], recv_sem=grecv.at[base + k - 1],
                device_id=target(k), device_id_type=MESH,
            ).wait_recv()
        value = seen[0]
        for k in range(1, count):
            value = value + seen[k]
        gram_copies += copies
        base += count - 1
    gram_ref[...] = value

    @pl.loop(0, UNITS)
    def _(u):
        g, c = u // CHUNKS, lax.rem(u, CHUNKS)
        for level in range(3):
            for copy in y_copies(level, g, c) + x_copies(level, g, c):
                copy.wait_send()

    for level in range(3):
        for g in range(GROUPS):
            for up in (False, True):
                z_copy(level, g, up).wait_send()
    for copy in gram_copies:
        copy.wait_send()


def solve_kernel(filt, gram_ref, out_hbm, factor_ref, out, out_sem):
    def entry(i, j):
        at = NORB * (i % SUB) + j
        return jnp.broadcast_to(gram_ref[i // SUB : i // SUB + 1, at : at + 1], (SUB, LX))

    lower, inverse = {}, {}
    for j in range(NORB):
        column = {i: entry(i, j) for i in range(j, NORB)}
        for k in range(j):
            for i in range(j, NORB):
                column[i] = column[i] - lower[i, k] * lower[j, k]
        root = jnp.sqrt(column[j])
        scale = F32(1) / root
        lower[j, j] = root
        for i in range(j + 1, NORB):
            lower[i, j] = column[i] * scale
        for k in range(j):
            total = lower[j, k] * inverse[k, k]
            for m in range(k + 1, j):
                total = total + lower[j, m] * inverse[m, k]
            inverse[j, k] = -(total * scale)
        inverse[j, j] = scale

    row = lax.broadcasted_iota(jnp.int32, (SUB, LX), 0)
    lane = lax.broadcasted_iota(jnp.int32, (SUB, LX), 1)
    at_row = [row == i for i in range(SUB)]

    def gather(entries):
        halves = []
        for half in range(GROUPS):
            rows = jnp.zeros((SUB, LX), F32)
            for i in range(SUB):
                line = jnp.zeros((SUB, LX), F32)
                for j in range(NORB):
                    if (half * SUB + i, j) in entries:
                        line = jnp.where(lane == j, entries[half * SUB + i, j], line)
                rows = jnp.where(at_row[i], line, rows)
            halves.append(rows)
        return jnp.concatenate(halves, axis=0)

    high, low = split(gather(inverse)[:, :NORB])
    lhs = jnp.concatenate([high, high, low], axis=1)

    flat = out.reshape(NORB * ROWS, LX)

    def out_copy(c):
        part = pl.ds(c * SLABS * LY, SLABS * LY)
        return pltpu.make_async_copy(out.at[:, part], out_hbm.at[:, part], out_sem.at[c])

    for c in range(CHUNKS):
        @pl.loop(0, SLABS)
        def _(s, c=c):
            z = c * SLABS + s
            wide = jnp.concatenate(
                [
                    jnp.concatenate([filt[g, z, y] for g in range(GROUPS)], axis=0)
                    for y in range(LY)
                ],
                axis=1,
            )
            high, low = split(wide)
            solved = jnp.dot(
                lhs, jnp.concatenate([high, low, high], axis=0), preferred_element_type=F32
            )
            for y in range(LY):
                flat[pl.ds(z * LY + y, NORB, stride=ROWS), :] = solved[:, y * LX : (y + 1) * LX]

        out_copy(c).start()
    factor_ref[...] = gather({(j, i): value for (i, j), value in lower.items()})[:, :NORB]
    for c in range(CHUNKS):
        out_copy(c).wait()


def on_device(orbitals, potential):
    hbm = pl.BlockSpec(memory_space=pltpu.HBM)
    vmem = pl.BlockSpec(memory_space=pltpu.VMEM)
    dma = pltpu.SemaphoreType.DMA
    sizes = {axis: lax.axis_size(axis) for axis in AXES}
    partners = sizes["gx"] * sizes["gy"] + sizes["gz"] - 2
    filtered, gram = pl.pallas_call(
        filter_kernel,
        name="filter_and_gram",
        out_shape=[
            jax.ShapeDtypeStruct((GROUPS, LZ, LY, SUB, LX), F32),
            jax.ShapeDtypeStruct((2, LX), F32),
        ],
        in_specs=[hbm] * 3,
        out_specs=[vmem, vmem],
        scratch_shapes=[
            pltpu.VMEM((NORB, ROWS, LX), F32),
            pltpu.VMEM((3, GROUPS, LZ + 2 * HALO, LY + 2 * HALO, SUB, LX), F32),
            pltpu.VMEM((3, GROUPS, LZ, SUB, LX), F32),
            pltpu.VMEM((3, GROUPS, LZ, SUB, LX), F32),
            pltpu.VMEM((3, GROUPS, LZ, SUB, LX), F32),
            pltpu.VMEM((LZ, LY, LX), F32),
            pltpu.VMEM((2 * LX, 2 * LX), BF16),
            pltpu.VMEM((NORB, LX), F32),
            pltpu.VMEM((sizes["gx"] * sizes["gy"], 2, LX), F32),
            pltpu.VMEM((sizes["gz"], 2, LX), F32),
            dma((UNITS,)),
            dma((2,)),
            dma((3, UNITS, 2)),
            dma((3, UNITS, 2)),
            dma((3, UNITS, 2)),
            dma((3, UNITS, 2)),
            dma((3, GROUPS, 2)),
            dma((3, GROUPS, 2)),
            dma((partners,)),
            dma((partners,)),
        ],
        compiler_params=pltpu.CompilerParams(
            collective_id=0, has_side_effects=True, vmem_limit_bytes=40 * 2**20
        ),
        cost_estimate=pl.CostEstimate(
            flops=10**9, bytes_accessed=5 * 2**20, transcendentals=0
        ),
    )(*[
        pltpu.with_memory_space_constraint(value, pltpu.HBM)
        for value in (
            orbitals.reshape(NORB, ROWS, LX), potential, jnp.asarray(x_weights())
        )
    ])
    solved, factor = pl.pallas_call(
        solve_kernel,
        name="solve",
        out_shape=[
            jax.ShapeDtypeStruct((NORB, ROWS, LX), F32),
            jax.ShapeDtypeStruct((NORB, NORB), F32),
        ],
        in_specs=[vmem, vmem],
        out_specs=[hbm, vmem],
        scratch_shapes=[
            pltpu.VMEM((NORB, ROWS, LX), F32),
            dma((CHUNKS,)),
        ],
        compiler_params=pltpu.CompilerParams(vmem_limit_bytes=24 * 2**20),
        cost_estimate=pl.CostEstimate(
            flops=10**8, bytes_accessed=4 * 2**20, transcendentals=0
        ),
    )(filtered, gram)
    return solved.reshape(NORB, LZ, LY, LX), factor


def solution(mesh):
    in_specs = (P(None, "gz", "gy", "gx"), P("gz", "gy", "gx"))
    out_specs = (P(None, "gz", "gy", "gx"), P())
    return jax.shard_map(
        on_device, mesh=mesh, in_specs=in_specs, out_specs=out_specs, check_vma=False
    )
```

time: 418 us -> 66.3 us (0.16); the launches traced: 412 us -> 66.2 us
  waiting for transfers between devices: 125 us -> 0 us
  other arithmetic: 109 us -> 0 us
  local copies, waits for them, and re-layouts: 68.6 us -> 0 us
  blocking collectives: 67.5 us -> 0 us
  Pallas kernels: 0 us -> 65.6 us
  starting transfers between devices: 30.8 us -> 0 us
  matrix products: 9.79 us -> 0 us
    ppermute x18 -> x0, waiting for transfers between devices: 125 us -> none  [the longest x9 87.6 us: padded_2(): lax.ppermute(lax.slice_in_dim(block, block.shape[dim] - width, None, axis...]
    psum x1 -> x0, blocking collectives: 67.5 us -> none  [on_device(): gram = lax.psum(local_gram, ('gx', 'gy', 'gz'))]
    pallas_call x0 -> x2, Pallas kernels: none -> 65.6 us  [the longest x1 60.3 us: on_device(): pl.pallas_call(filter_kernel, name='filter_and_gram', out_shape=[jax.Shap...]
    sub x2 -> x0, other arithmetic: 48.4 us -> none  [the longest x1 24.5 us: on_device(): 2.0 * (hamilton(rim_layers(level_two), potential) - CENTRE * level_two)]
    ppermute x12 -> x0, local copies, waits for them, and re-layouts: 31.5 us -> none  [the longest x6 17.4 us: padded_2(): lax.ppermute(lax.slice_in_dim(block, 0, width, axis=dim), axis, backward)]
    ppermute x18 -> x0, starting transfers between devices: 30.8 us -> none  [the longest x9 19.4 us: padded_2(): lax.ppermute(lax.slice_in_dim(block, 0, width, axis=dim), axis, backward)]
    concatenate x6 -> x0, other arithmetic: 25 us -> none  [padded_2(): block = jnp.concatenate([low, block, high], axis=dim)]
    div x2 -> x0, other arithmetic: 24.3 us -> none  [the longest x1 24.3 us: on_device(): (hamilton(rim_layers(orbitals), potential) - CENTRE * orbitals) / HALF_WIDTH]
  transfers between devices with their start and end apart: 18 -> 0, of which waited for: 11 -> 0; matrix products, arithmetic and copies ran while one was open for 11% -> 0% of each run, Pallas kernels for 0% -> 0%
where the time goes in v1:
time: 66.3 us; the launch traced here: 66.2 us
  Pallas kernels  65.6 us (99%)
    pallas_call x1, Pallas kernels, on_device(): pl.pallas_call(filter_kernel, name='filter_and_gram', out_shape=[jax.Shap...  60.3 us
    pallas_call x1, Pallas kernels, on_device(): pl.pallas_call(solve_kernel, name='solve', out_shape=[jax.ShapeDtypeStruc...  5.3 us

profile of v1, /device:TPU:1, one launch (start us, length us, event | category | flops | bytes accessed | tf_op | source)
XLA Modules:
  0.0 66.2 jit_solution(3998078632626325705)
XLA Ops:
  0.6 60.3 %filter_and_gram.1 = (f32[2,16,16,8,128]{4,3,2,1,0:T(8,128)S(1)}, f32[2,128]{1,0:T(2,128)S(1)}) custom-call(f32[16,256,128]{2,1,0:T(8,128)} %bitcast.2, f32[16,16,128]{2,1,0:T(8,128)} %pot_hbm.1, bf16[256,256]{1,0:T(8,128)(2,1)} %constant.2.clone.w_hbm), custom_call_target="tpu_custom_call" | custom-call | flops 1000000000 | bytes 5242880 | tf_op jit(solution)/shard_map/filter_and_gram/pallas_call | solution.py:403
  60.9 5.3 %solve.1 = (f32[16,256,128]{2,1,0:T(8,128)}, f32[16,16]{1,0:T(8,128)}) custom-call(f32[2,16,16,8,128]{4,3,2,1,0:T(8,128)S(1)} %get-tuple-element.6.filt, f32[2,128]{1,0:T(2,128)S(1)} %get-tuple-element.7.gram_ref), custom_call_target="tpu_custom_call" | custom-call | flops 100000000 | bytes 4194304 | tf_op jit(solution)/shard_map/solve/pallas_call | solution.py:446

commit v2 on v1

--- a/solution.py
+++ b/solution.py
@@ -20,6 +20,8 @@
 SLABS = 4
 CHUNKS = LZ // SLABS
 UNITS = GROUPS * CHUNKS
+QUAD = 8 * HALO
+UNROLL = 4
 ROWS = LZ * LY
 CELLS = 4194304
 F32, BF16 = jnp.float32, jnp.bfloat16
@@ -30,12 +32,15 @@
 def x_weights():
     places = np.concatenate([np.arange(LX), np.arange(-HALO, 0), np.arange(LX, LX + HALO)])
     away = np.abs(places[:, None] - np.arange(LX)[None, :])
-    full = np.zeros((2 * LX, LX), np.float32)
+    full = np.zeros((LX + 2 * HALO, LX), np.float32)
     for k in range(1, HALO + 1):
-        full[: len(places)][away == k] = np.float32(TAPS[k])
+        full[away == k] = np.float32(TAPS[k])
     high = full.astype(ml_dtypes.bfloat16)
     low = (full - high.astype(np.float32)).astype(ml_dtypes.bfloat16)
-    return np.concatenate([high, low], axis=1)
+    halo = np.zeros((LX, LX), ml_dtypes.bfloat16)
+    for start, part in ((0, high), (QUAD, high), (2 * QUAD, low)):
+        halo[start : start + 2 * HALO] = part[LX:]
+    return np.concatenate([high[:LX], halo, high[:LX], low[:LX]], axis=0)
 
 
 def split(value):
@@ -45,9 +50,10 @@
 
 def filter_kernel(
     orb_hbm, pot_hbm, w_hbm, last, gram_ref,
-    load, buf, pack, from_left, from_right, pv, w_ref, part, seen_xy, seen_z,
+    load, buf0, buf1, buf2, pack0, pack1, pack2, from_left, from_right, pv, w_ref, part, seen_xy, seen_z,
     load_sem, small_sem, ysend, yrecv, xsend, xrecv, zsend, zrecv, gsend, grecv,
 ):
+    bufs, packs = (buf0, buf1, buf2), (pack0, pack1, pack2)
     sizes = {axis: lax.axis_size(axis) for axis in AXES}
     here = {axis: lax.axis_index(axis) for axis in AXES}
 
@@ -91,7 +97,7 @@
 
     def y_copies(level, g, c):
         u, zs = g * CHUNKS + c, pl.ds(HALO + c * SLABS, SLABS)
-        level_buf = buf.at[level, g, zs]
+        level_buf = bufs[level].at[g, zs]
         return [
             remote(
                 level_buf.at[:, pl.ds(LY, HALO)], level_buf.at[:, pl.ds(0, HALO)],
@@ -107,11 +113,11 @@
         u, zs = g * CHUNKS + c, pl.ds(c * SLABS, SLABS)
         return [
             remote(
-                pack.at[level, g, zs], from_left.at[level, g, zs],
+                packs[level].at[g, zs], from_left.at[level, g, zs],
                 xsend.at[level, u, 0], xrecv.at[level, u, 0], "gx", 1,
             ),
             remote(
-                pack.at[level, g, zs], from_right.at[level, g, zs],
+                packs[level].at[g, zs], from_right.at[level, g, zs],
                 xsend.at[level, u, 1], xrecv.at[level, u, 1], "gx", -1,
             ),
         ]
@@ -121,7 +127,8 @@
         src, dst = (LZ, 0) if up else (HALO, HALO + LZ)
         i = 0 if up else 1
         return remote(
-            buf.at[level, g, pl.ds(src, HALO), inner], buf.at[level, g, pl.ds(dst, HALO), inner],
+            bufs[level].at[g, pl.ds(src, HALO), inner],
+            bufs[level].at[g, pl.ds(dst, HALO), inner],
             zsend.at[level, g, i], zrecv.at[level, g, i], "gz", 1 if up else -1,
         )
 
@@ -155,15 +162,15 @@
     def start_unit(g, c):
         load_copy(g, c).wait()
 
-        @pl.loop(0, SLABS)
+        @pl.loop(0, SLABS, unroll=UNROLL)
         def _(s):
             z = c * SLABS + s
             values = []
             for y in range(LY):
                 v = flat[pl.ds(g * SUB * ROWS + z * LY + y, SUB, stride=ROWS), :]
-                buf[0, g, HALO + z, HALO + y] = v
+                buf0[g, HALO + z, HALO + y] = v
                 values.append(v)
-            pack[0, g, z] = pack_edges(values)
+            pack0[g, z] = pack_edges(values)
 
     start_unit(0, 0)
     pl.semaphore_wait(barrier, len(others))
@@ -180,28 +187,36 @@
     pv[...] = pv[...] * F32(0.1) + F32(3.0 * TAPS[0] - 2.3)
 
     def stencil(level, g, z):
-        w = w_ref[...]
+        buf = bufs[level]
         edges = jnp.where(
             lax.rem(lane, 2 * HALO) < HALO, from_left[level, g, z], from_right[level, g, z]
         )
-        centre = [buf[level, g, HALO + z, HALO + y] for y in range(LY)]
-        rows = jnp.concatenate(centre, axis=0)
-        halo = jnp.concatenate(
-            [pltpu.roll(edges, (LX - 2 * HALO * y) % LX, 1) for y in range(LY)], axis=0
-        )
-        high, low = split(jnp.concatenate([rows, halo], axis=1))
-        both = jnp.dot(high, w, preferred_element_type=F32)
-        along_x = (
-            jnp.dot(low, w[:, :LX], preferred_element_type=F32) + both[:, :LX] + both[:, LX:]
-        )
+        edge_high = edges.astype(BF16).astype(F32)
+        parts = (
+            edge_high,
+            pltpu.roll(edges - edge_high, QUAD, 1),
+            pltpu.roll(edge_high, 2 * QUAD, 1),
+        )
+        halo = []
+        for quad in range(LX // QUAD):
+            own = parts[2]
+            for i in (1, 0):
+                own = jnp.where(lane // QUAD == (quad + i) % (LX // QUAD), parts[i], own)
+            for y in range(QUAD // 8 * quad, QUAD // 8 * (quad + 1)):
+                halo.append(pltpu.roll(own, (LX - 2 * HALO * y) % LX, 1))
+        centre = [buf[g, HALO + z, HALO + y] for y in range(LY)]
+        high, low = split(jnp.concatenate(centre, axis=0))
+        rows = jnp.concatenate(
+            [high, jnp.concatenate(halo, axis=0).astype(BF16), low, high], axis=1
+        )
+        along_x = jnp.dot(rows, w_ref[...], preferred_element_type=F32)
         out = []
         for y in range(LY):
-            here_v = centre[y]
-            total = pv[z, pl.ds(y, 1), :] * here_v + along_x[y * SUB : (y + 1) * SUB]
+            total = pv[z, pl.ds(y, 1), :] * centre[y] + along_x[y * SUB : (y + 1) * SUB]
             for k in range(1, HALO + 1):
                 around = (
-                    buf[level, g, HALO + z + k, HALO + y] + buf[level, g, HALO + z - k, HALO + y]
-                ) + (buf[level, g, HALO + z, HALO + y + k] + buf[level, g, HALO + z, HALO + y - k])
+                    buf[g, HALO + z + k, HALO + y] + buf[g, HALO + z - k, HALO + y]
+                ) + (buf[g, HALO + z, HALO + y + k] + buf[g, HALO + z, HALO + y - k])
                 total = total + F32(TAPS[k]) * around
             out.append(total)
         return out
@@ -225,17 +240,17 @@
             g, c = u // CHUNKS, lax.rem(u, CHUNKS)
             wait_halos(level - 1, g, c)
 
-            @pl.loop(0, SLABS)
+            @pl.loop(0, SLABS, unroll=UNROLL)
             def _(s):
                 z = c * SLABS + s
                 new = stencil(level - 1, g, z)
                 if level == 1:
                     new = [F32(0.5) * v for v in new]
                 else:
-                    new = [v - buf[0, g, HALO + z, HALO + y] for y, v in enumerate(new)]
+                    new = [v - buf0[g, HALO + z, HALO + y] for y, v in enumerate(new)]
                 for y in range(LY):
-                    buf[level, g, HALO + z, HALO + y] = new[y]
-                pack[level, g, z] = pack_edges(new)
+                    bufs[level][g, HALO + z, HALO + y] = new[y]
+                packs[level][g, z] = pack_edges(new)
 
             send(level, g, c)
 
@@ -246,16 +261,16 @@
         g, c = u // CHUNKS, lax.rem(u, CHUNKS)
         wait_halos(2, g, c)
 
-        @pl.loop(0, SLABS)
+        @pl.loop(0, SLABS, unroll=UNROLL)
         def _(s):
             z = c * SLABS + s
             new = stencil(2, g, z)
             for y in range(LY):
-                last[g, z, y] = new[y] - buf[1, g, HALO + z, HALO + y]
+                last[g, z, y] = new[y] - buf1[g, HALO + z, HALO + y]
 
         @pl.when(g == GROUPS - 1)
         def _():
-            @pl.loop(0, SLABS)
+            @pl.loop(0, SLABS, unroll=UNROLL)
             def _(s):
                 z = c * SLABS + s
                 wide = jnp.concatenate(
@@ -273,52 +288,44 @@
                 four = quad[:NORB] + quad[NORB:]
                 part[:, :NORB] += four[:, :NORB] + four[:, NORB:]
 
-    gram_copies = []
+    def wait_sends():
+        @pl.loop(0, UNITS)
+        def _(u):
+            g, c = u // CHUNKS, lax.rem(u, CHUNKS)
+            for level in range(3):
+                for copy in y_copies(level, g, c) + x_copies(level, g, c):
+                    copy.wait_send()
+
+        for level in range(3):
+            for g in range(GROUPS):
+                for up in (False, True):
+                    z_copy(level, g, up).wait_send()
+
     moved = pltpu.roll(part[...] * F32(1.0 / CELLS), 0, 1, stride=NORB, stride_axis=0)
     value = jnp.sum(moved.reshape(2, SUB, LX), axis=1)
     plane = sizes["gx"] * sizes["gy"]
-    base = 0
-    for seen, count, mine, target in (
+    stages = (
         (seen_xy, plane, here["gx"] * sizes["gy"] + here["gy"], in_plane),
         (seen_z, sizes["gz"], here["gz"], in_column),
-    ):
+    )
+    for stage, (seen, count, mine, target) in enumerate(stages):
         seen[mine] = value
-        copies = []
         for k in range(1, count):
-            copies.append(
-                pltpu.make_async_remote_copy(
-                    src_ref=seen.at[mine], dst_ref=seen.at[mine], send_sem=gsend.at[base + k - 1],
-                    recv_sem=grecv.at[base + k - 1], device_id=target(k), device_id_type=MESH,
-                )
-            )
-            copies[-1].start()
-        for k in range(1, count):
-            came_from = lax.rem(mine + count - k, count)
             pltpu.make_async_remote_copy(
-                src_ref=seen.at[came_from], dst_ref=seen.at[came_from],
-                send_sem=gsend.at[base + k - 1], recv_sem=grecv.at[base + k - 1],
-                device_id=target(k), device_id_type=MESH,
-            ).wait_recv()
+                src_ref=seen.at[mine], dst_ref=seen.at[mine], send_sem=gsend.at[stage],
+                recv_sem=grecv.at[stage], device_id=target(k), device_id_type=MESH,
+            ).start()
+        if stage == 0:
+            wait_sends()
+        others = seen.at[pl.ds(0, count - 1)]
+        pltpu.make_async_copy(others, others, grecv.at[stage]).wait()
         value = seen[0]
         for k in range(1, count):
             value = value + seen[k]
-        gram_copies += copies
-        base += count - 1
     gram_ref[...] = value
-
-    @pl.loop(0, UNITS)
-    def _(u):
-        g, c = u // CHUNKS, lax.rem(u, CHUNKS)
-        for level in range(3):
-            for copy in y_copies(level, g, c) + x_copies(level, g, c):
-                copy.wait_send()
-
-    for level in range(3):
-        for g in range(GROUPS):
-            for up in (False, True):
-                z_copy(level, g, up).wait_send()
-    for copy in gram_copies:
-        copy.wait_send()
+    for stage, (seen, count, _, _) in enumerate(stages):
+        others = seen.at[pl.ds(0, count - 1)]
+        pltpu.make_async_copy(others, others, gsend.at[stage]).wait()
 
 
 def solve_kernel(filt, gram_ref, out_hbm, factor_ref, out, out_sem):
@@ -371,7 +378,7 @@
         return pltpu.make_async_copy(out.at[:, part], out_hbm.at[:, part], out_sem.at[c])
 
     for c in range(CHUNKS):
-        @pl.loop(0, SLABS)
+        @pl.loop(0, SLABS, unroll=UNROLL)
         def _(s, c=c):
             z = c * SLABS + s
             wide = jnp.concatenate(
@@ -399,7 +406,6 @@
     vmem = pl.BlockSpec(memory_space=pltpu.VMEM)
     dma = pltpu.SemaphoreType.DMA
     sizes = {axis: lax.axis_size(axis) for axis in AXES}
-    partners = sizes["gx"] * sizes["gy"] + sizes["gz"] - 2
     filtered, gram = pl.pallas_call(
         filter_kernel,
         name="filter_and_gram",
@@ -411,12 +417,11 @@
         out_specs=[vmem, vmem],
         scratch_shapes=[
             pltpu.VMEM((NORB, ROWS, LX), F32),
-            pltpu.VMEM((3, GROUPS, LZ + 2 * HALO, LY + 2 * HALO, SUB, LX), F32),
-            pltpu.VMEM((3, GROUPS, LZ, SUB, LX), F32),
-            pltpu.VMEM((3, GROUPS, LZ, SUB, LX), F32),
-            pltpu.VMEM((3, GROUPS, LZ, SUB, LX), F32),
+            *[pltpu.VMEM((GROUPS, LZ + 2 * HALO, LY + 2 * HALO, SUB, LX), F32)] * 3,
+            *[pltpu.VMEM((GROUPS, LZ, SUB, LX), F32)] * 3,
+            *[pltpu.VMEM((3, GROUPS, LZ, SUB, LX), F32)] * 2,
             pltpu.VMEM((LZ, LY, LX), F32),
-            pltpu.VMEM((2 * LX, 2 * LX), BF16),
+            pltpu.VMEM((4 * LX, LX), BF16),
             pltpu.VMEM((NORB, LX), F32),
             pltpu.VMEM((sizes["gx"] * sizes["gy"], 2, LX), F32),
             pltpu.VMEM((sizes["gz"], 2, LX), F32),
@@ -428,8 +433,8 @@
             dma((3, UNITS, 2)),
             dma((3, GROUPS, 2)),
             dma((3, GROUPS, 2)),
-            dma((partners,)),
-            dma((partners,)),
+            dma((2,)),
+            dma((2,)),
         ],
         compiler_params=pltpu.CompilerParams(
             collective_id=0, has_side_effects=True, vmem_limit_bytes=40 * 2**20

time: 66.3 us -> 60 us (0.905)
  Pallas kernels: 65.6 us -> 59.2 us
    pallas_call x1, Pallas kernels: 60.3 us -> 55.7 us  [on_device(): pl.pallas_call(filter_kernel, name='filter_and_gram', out_shape=[jax.Shap...]
    pallas_call x1, Pallas kernels: 5.3 us -> 3.46 us  [on_device(): pl.pallas_call(solve_kernel, name='solve', out_shape=[jax.ShapeDtypeStruc...]
where the time goes in v2:
time: 60 us; the launch traced here: 59.8 us
  Pallas kernels  59.2 us (99%)
  between operations  0.64 us (1%)
    pallas_call x1, Pallas kernels, on_device(): pl.pallas_call(filter_kernel, name='filter_and_gram', out_shape=[jax.Shap...  55.7 us
    pallas_call x1, Pallas kernels, on_device(): pl.pallas_call(solve_kernel, name='solve', out_shape=[jax.ShapeDtypeStruc...  3.46 us

profile of v2, /device:TPU:1, one launch (start us, length us, event | category | flops | bytes accessed | tf_op | source)
XLA Modules:
  0.0 59.8 jit_solution(3522920267142292753)
XLA Ops:
  0.6 55.7 %filter_and_gram.1 = (f32[2,16,16,8,128]{4,3,2,1,0:T(8,128)S(1)}, f32[2,128]{1,0:T(2,128)S(1)}) custom-call(f32[16,256,128]{2,1,0:T(8,128)} %bitcast.2, f32[16,16,128]{2,1,0:T(8,128)} %pot_hbm.1, bf16[512,128]{1,0:T(8,128)(2,1)} %constant.2.clone.w_hbm), custom_call_target="tpu_custom_call" | custom-call | flops 1000000000 | bytes 5242880 | tf_op jit(solution)/shard_map/filter_and_gram/pallas_call | solution.py:409
  56.4 3.5 %solve.1 = (f32[16,256,128]{2,1,0:T(8,128)}, f32[16,16]{1,0:T(8,128)}) custom-call(f32[2,16,16,8,128]{4,3,2,1,0:T(8,128)S(1)} %get-tuple-element.6.filt, f32[2,128]{1,0:T(2,128)S(1)} %get-tuple-element.7.gram_ref), custom_call_target="tpu_custom_call" | custom-call | flops 100000000 | bytes 4194304 | tf_op jit(solution)/shard_map/solve/pallas_call | solution.py:451

commit v3 on v2

--- a/solution.py
+++ b/solution.py
@@ -22,6 +22,7 @@
 UNITS = GROUPS * CHUNKS
 QUAD = 8 * HALO
 UNROLL = 4
+STEP = 2
 ROWS = LZ * LY
 CELLS = 4194304
 F32, BF16 = jnp.float32, jnp.bfloat16
@@ -60,6 +61,18 @@
     def at(axis, step):
         return {axis: lax.rem(here[axis] + (step + sizes[axis]), sizes[axis])}
 
+    neighbours = [(axis, step) for axis in ("gy", "gz", "gx") for step in (1, -1)]
+    barrier = pltpu.get_barrier_semaphore()
+    for axis, step in neighbours:
+        pl.semaphore_signal(barrier, inc=1, device_id=at(axis, step), device_id_type=MESH)
+
+    def in_plane(k):
+        other = lax.rem(here["gx"] * sizes["gy"] + here["gy"] + k, sizes["gx"] * sizes["gy"])
+        return {"gx": other // sizes["gy"], "gy": lax.rem(other, sizes["gy"])}
+
+    def in_column(k):
+        return at("gz", k)
+
     def load_copy(g, c):
         part = (pl.ds(g * SUB, SUB), pl.ds(c * SLABS * LY, SLABS * LY))
         return pltpu.make_async_copy(
@@ -75,19 +88,6 @@
             load_copy(g, c).start()
     for copy in small:
         copy.start()
-
-    def in_plane(k):
-        other = lax.rem(here["gx"] * sizes["gy"] + here["gy"] + k, sizes["gx"] * sizes["gy"])
-        return {"gx": other // sizes["gy"], "gy": lax.rem(other, sizes["gy"])}
-
-    def in_column(k):
-        return at("gz", k)
-
-    others = [in_plane(k) for k in range(1, sizes["gx"] * sizes["gy"])]
-    others += [in_column(k) for k in range(1, sizes["gz"])]
-    barrier = pltpu.get_barrier_semaphore()
-    for device in others:
-        pl.semaphore_signal(barrier, inc=1, device_id=device, device_id_type=MESH)
 
     def remote(src, dst, send_sem, recv_sem, axis, step):
         return pltpu.make_async_remote_copy(
@@ -173,7 +173,7 @@
             pack0[g, z] = pack_edges(values)
 
     start_unit(0, 0)
-    pl.semaphore_wait(barrier, len(others))
+    pl.semaphore_wait(barrier, len(neighbours))
     send(0, 0, 0)
 
     @pl.loop(1, UNITS)
@@ -333,7 +333,9 @@
         at = NORB * (i % SUB) + j
         return jnp.broadcast_to(gram_ref[i // SUB : i // SUB + 1, at : at + 1], (SUB, LX))
 
-    lower, inverse = {}, {}
+    row = lax.broadcasted_iota(jnp.int32, (SUB, LX), 0)
+    lane = lax.broadcasted_iota(jnp.int32, (SUB, LX), 1)
+    lower, inverse = {}, []
     for j in range(NORB):
         column = {i: entry(i, j) for i in range(j, NORB)}
         for k in range(j):
@@ -344,43 +346,39 @@
         lower[j, j] = root
         for i in range(j + 1, NORB):
             lower[i, j] = column[i] * scale
-        for k in range(j):
-            total = lower[j, k] * inverse[k, k]
-            for m in range(k + 1, j):
-                total = total + lower[j, m] * inverse[m, k]
-            inverse[j, k] = -(total * scale)
-        inverse[j, j] = scale
-
-    row = lax.broadcasted_iota(jnp.int32, (SUB, LX), 0)
-    lane = lax.broadcasted_iota(jnp.int32, (SUB, LX), 1)
-    at_row = [row == i for i in range(SUB)]
-
-    def gather(entries):
+        line = jnp.where(lane == j, F32(1), F32(0))
+        for m in range(j):
+            line = line - lower[j, m] * inverse[m]
+        inverse.append(line * scale)
+
+    def stack(lines):
         halves = []
         for half in range(GROUPS):
-            rows = jnp.zeros((SUB, LX), F32)
-            for i in range(SUB):
-                line = jnp.zeros((SUB, LX), F32)
-                for j in range(NORB):
-                    if (half * SUB + i, j) in entries:
-                        line = jnp.where(lane == j, entries[half * SUB + i, j], line)
-                rows = jnp.where(at_row[i], line, rows)
+            rows = lines[half * SUB]
+            for i in range(1, SUB):
+                rows = jnp.where(row == i, lines[half * SUB + i], rows)
             halves.append(rows)
         return jnp.concatenate(halves, axis=0)
 
-    high, low = split(gather(inverse)[:, :NORB])
+    def gather(entries):
+        lines = []
+        for i in range(NORB):
+            line = jnp.zeros((SUB, LX), F32)
+            for j in range(NORB):
+                if (i, j) in entries:
+                    line = jnp.where(lane == j, entries[i, j], line)
+            lines.append(line)
+        return stack(lines)
+
+    high, low = split(stack(inverse)[:, :NORB])
     lhs = jnp.concatenate([high, high, low], axis=1)
 
-    flat = out.reshape(NORB * ROWS, LX)
-
     def out_copy(c):
-        part = pl.ds(c * SLABS * LY, SLABS * LY)
+        part = pl.ds(c * STEP * LY, STEP * LY)
         return pltpu.make_async_copy(out.at[:, part], out_hbm.at[:, part], out_sem.at[c])
 
-    for c in range(CHUNKS):
-        @pl.loop(0, SLABS, unroll=UNROLL)
-        def _(s, c=c):
-            z = c * SLABS + s
+    for c in range(LZ // STEP):
+        for z in range(c * STEP, (c + 1) * STEP):
             wide = jnp.concatenate(
                 [
                     jnp.concatenate([filt[g, z, y] for g in range(GROUPS)], axis=0)
@@ -392,12 +390,20 @@
             solved = jnp.dot(
                 lhs, jnp.concatenate([high, low, high], axis=0), preferred_element_type=F32
             )
-            for y in range(LY):
-                flat[pl.ds(z * LY + y, NORB, stride=ROWS), :] = solved[:, y * LX : (y + 1) * LX]
-
+            for g in range(GROUPS):
+                for start in range(0, LY, SUB):
+                    block = jnp.stack(
+                        [
+                            solved[g * SUB : (g + 1) * SUB, y * LX : (y + 1) * LX]
+                            for y in range(start, start + SUB)
+                        ]
+                    )
+                    out[pl.ds(g * SUB, SUB), pl.ds(z * LY + start, SUB), :] = jnp.swapaxes(
+                        block, 0, 1
+                    )
         out_copy(c).start()
     factor_ref[...] = gather({(j, i): value for (i, j), value in lower.items()})[:, :NORB]
-    for c in range(CHUNKS):
+    for c in range(LZ // STEP):
         out_copy(c).wait()
 
 
@@ -459,7 +465,7 @@
         out_specs=[hbm, vmem],
         scratch_shapes=[
             pltpu.VMEM((NORB, ROWS, LX), F32),
-            dma((CHUNKS,)),
+            dma((LZ // STEP,)),
         ],
         compiler_params=pltpu.CompilerParams(vmem_limit_bytes=24 * 2**20),
         cost_estimate=pl.CostEstimate(

time: 60 us -> 57.8 us (0.963)
  Pallas kernels: 59.2 us -> 57.1 us
    pallas_call x1, Pallas kernels: 55.7 us -> 54.4 us  [on_device(): pl.pallas_call(filter_kernel, name='filter_and_gram', out_shape=[jax.Shap...]
    pallas_call x1, Pallas kernels: 3.46 us -> 2.69 us  [on_device(): pl.pallas_call(solve_kernel, name='solve', out_shape=[jax.ShapeDtypeStruc...]
where the time goes in v3:
time: 57.8 us; the launch traced here: 57.7 us
  Pallas kernels  57.1 us (99%)
  between operations  0.64 us (1%)
    pallas_call x1, Pallas kernels, on_device(): pl.pallas_call(filter_kernel, name='filter_and_gram', out_shape=[jax.Shap...  54.4 us
    pallas_call x1, Pallas kernels, on_device(): pl.pallas_call(solve_kernel, name='solve', out_shape=[jax.ShapeDtypeStruc...  2.69 us

profile of v3, /device:TPU:1, one launch (start us, length us, event | category | flops | bytes accessed | tf_op | source)
XLA Modules:
  0.0 57.7 jit_solution(8866883664810056051)
XLA Ops:
  0.6 54.4 %filter_and_gram.1 = (f32[2,16,16,8,128]{4,3,2,1,0:T(8,128)S(1)}, f32[2,128]{1,0:T(2,128)S(1)}) custom-call(f32[16,256,128]{2,1,0:T(8,128)} %bitcast.2, f32[16,16,128]{2,1,0:T(8,128)} %pot_hbm.1, bf16[512,128]{1,0:T(8,128)(2,1)} %constant.2.clone.w_hbm), custom_call_target="tpu_custom_call" | custom-call | flops 1000000000 | bytes 5242880 | tf_op jit(solution)/shard_map/filter_and_gram/pallas_call | solution.py:415
  55.0 2.7 %solve.1 = (f32[16,256,128]{2,1,0:T(8,128)}, f32[16,16]{1,0:T(8,128)}) custom-call(f32[2,16,16,8,128]{4,3,2,1,0:T(8,128)S(1)} %get-tuple-element.6.filt, f32[2,128]{1,0:T(2,128)S(1)} %get-tuple-element.7.gram_ref), custom_call_target="tpu_custom_call" | custom-call | flops 100000000 | bytes 4194304 | tf_op jit(solution)/shard_map/solve/pallas_call | solution.py:457

commit v4 on v3

--- a/solution.py
+++ b/solution.py
@@ -51,7 +51,7 @@
 
 def filter_kernel(
     orb_hbm, pot_hbm, w_hbm, last, gram_ref,
-    load, buf0, buf1, buf2, pack0, pack1, pack2, from_left, from_right, pv, w_ref, part, seen_xy, seen_z,
+    load, buf0, buf1, buf2, pack0, pack1, pack2, from_left, from_right, pv, w_ref, part, pair, seen, word,
     load_sem, small_sem, ysend, yrecv, xsend, xrecv, zsend, zrecv, gsend, grecv,
 ):
     bufs, packs = (buf0, buf1, buf2), (pack0, pack1, pack2)
@@ -65,13 +65,6 @@
     barrier = pltpu.get_barrier_semaphore()
     for axis, step in neighbours:
         pl.semaphore_signal(barrier, inc=1, device_id=at(axis, step), device_id_type=MESH)
-
-    def in_plane(k):
-        other = lax.rem(here["gx"] * sizes["gy"] + here["gy"] + k, sizes["gx"] * sizes["gy"])
-        return {"gx": other // sizes["gy"], "gy": lax.rem(other, sizes["gy"])}
-
-    def in_column(k):
-        return at("gz", k)
 
     def load_copy(g, c):
         part = (pl.ds(g * SUB, SUB), pl.ds(c * SLABS * LY, SLABS * LY))
@@ -233,12 +226,39 @@
         def _():
             z_copy(level, g, False).wait_recv()
 
+    core = lax.rem(here["gz"], 2)
+    layers = sizes["gz"] // 2
+    rounds = (
+        [("gx", d) for d in range(1, sizes["gx"])],
+        [("gy", d) for d in range(1, sizes["gy"])],
+        [("gz", 2), ("gz", -2)],
+        [("gz", d) for d in range(4, sizes["gz"] - 3, 2)],
+    )
+
+    def tell(i):
+        for axis, step in rounds[i]:
+            pl.semaphore_signal(
+                word.at[i], inc=1, device_id=at(axis, step), device_id_type=MESH
+            )
+
+    def hear(i):
+        pl.semaphore_wait(word.at[i], len(rounds[i]))
+
     for level in (1, 2):
+        if level == 2:
+            tell(0)
 
         @pl.loop(0, UNITS)
         def _(u, level=level):
             g, c = u // CHUNKS, lax.rem(u, CHUNKS)
             wait_halos(level - 1, g, c)
+
+            if level == 2:
+
+                @pl.when(u == CHUNKS)
+                def _():
+                    hear(0)
+                    tell(1)
 
             @pl.loop(0, SLABS, unroll=UNROLL)
             def _(s):
@@ -254,12 +274,19 @@
 
             send(level, g, c)
 
+    hear(1)
+    tell(2)
     part[...] = jnp.zeros_like(part)
 
     @pl.loop(0, UNITS)
     def _(u):
         g, c = u // CHUNKS, lax.rem(u, CHUNKS)
         wait_halos(2, g, c)
+
+        @pl.when(u == CHUNKS)
+        def _():
+            hear(2)
+            tell(3)
 
         @pl.loop(0, SLABS, unroll=UNROLL)
         def _(s):
@@ -301,31 +328,43 @@
                 for up in (False, True):
                     z_copy(level, g, up).wait_send()
 
+    hear(3)
     moved = pltpu.roll(part[...] * F32(1.0 / CELLS), 0, 1, stride=NORB, stride_axis=0)
-    value = jnp.sum(moved.reshape(2, SUB, LX), axis=1)
-    plane = sizes["gx"] * sizes["gy"]
-    stages = (
-        (seen_xy, plane, here["gx"] * sizes["gy"] + here["gy"], in_plane),
-        (seen_z, sizes["gz"], here["gz"], in_column),
-    )
-    for stage, (seen, count, mine, target) in enumerate(stages):
-        seen[mine] = value
-        for k in range(1, count):
-            pltpu.make_async_remote_copy(
-                src_ref=seen.at[mine], dst_ref=seen.at[mine], send_sem=gsend.at[stage],
-                recv_sem=grecv.at[stage], device_id=target(k), device_id_type=MESH,
-            ).start()
-        if stage == 0:
-            wait_sends()
-        others = seen.at[pl.ds(0, count - 1)]
-        pltpu.make_async_copy(others, others, grecv.at[stage]).wait()
-        value = seen[0]
-        for k in range(1, count):
-            value = value + seen[k]
+    pair[0] = jnp.sum(moved.reshape(2, SUB, LX), axis=1)
+    to_core = remote(pair.at[0], pair.at[1], gsend.at[0], grecv.at[0], "gz", 1 - 2 * core)
+    to_core.start()
+    wait_sends()
+    to_core.wait_recv()
+    mine = (here["gx"] * sizes["gy"] + here["gy"]) * layers + here["gz"] // 2
+    seen[mine] = pair[0] + pair[1]
+    offsets = [
+        (dx, dy, dz)
+        for dx in range(sizes["gx"])
+        for dy in range(sizes["gy"])
+        for dz in range(layers)
+    ][1:]
+    ring = {"gx": sizes["gx"], "gy": sizes["gy"], "gz": layers}
+
+    def hops(offset):
+        return sum(min(d, n - d) for d, n in zip(offset, ring.values()))
+
+    along = {axis: [at(axis, d * (2 if axis == "gz" else 1)) for d in range(ring[axis])] for axis in AXES}
+    for offset in sorted(offsets, key=hops, reverse=True):
+        pltpu.make_async_remote_copy(
+            src_ref=seen.at[mine], dst_ref=seen.at[mine], send_sem=gsend.at[1],
+            recv_sem=grecv.at[1],
+            device_id={axis: along[axis][d] for axis, d in zip(AXES, offset)},
+            device_id_type=MESH,
+        ).start()
+    others = seen.at[pl.ds(0, len(offsets))]
+    pltpu.make_async_copy(others, others, grecv.at[1]).wait()
+    terms = [seen[k] for k in range(len(offsets) + 1)]
+    while len(terms) > 1:
+        terms = [a + b for a, b in zip(terms[::2], terms[1::2])]
+    value = terms[0]
     gram_ref[...] = value
-    for stage, (seen, count, _, _) in enumerate(stages):
-        others = seen.at[pl.ds(0, count - 1)]
-        pltpu.make_async_copy(others, others, gsend.at[stage]).wait()
+    to_core.wait_send()
+    pltpu.make_async_copy(others, others, gsend.at[1]).wait()
 
 
 def solve_kernel(filt, gram_ref, out_hbm, factor_ref, out, out_sem):
@@ -429,8 +468,9 @@
             pltpu.VMEM((LZ, LY, LX), F32),
             pltpu.VMEM((4 * LX, LX), BF16),
             pltpu.VMEM((NORB, LX), F32),
-            pltpu.VMEM((sizes["gx"] * sizes["gy"], 2, LX), F32),
-            pltpu.VMEM((sizes["gz"], 2, LX), F32),
+            pltpu.VMEM((2, 2, LX), F32),
+            pltpu.VMEM((sizes["gx"] * sizes["gy"] * sizes["gz"] // 2, 2, LX), F32),
+            pltpu.SemaphoreType.REGULAR((4,)),
             dma((UNITS,)),
             dma((2,)),
             dma((3, UNITS, 2)),

time: 57.8 us -> 56 us (0.969)
  Pallas kernels: 57.1 us -> 55.3 us
    pallas_call x1, Pallas kernels: 54.4 us -> 52.6 us  [on_device(): pl.pallas_call(filter_kernel, name='filter_and_gram', out_shape=[jax.Shap...]
where the time goes in v4:
time: 56 us; the launch traced here: 55.9 us
  Pallas kernels  55.3 us (99%)
  between operations  0.64 us (1%)
    pallas_call x1, Pallas kernels, on_device(): pl.pallas_call(filter_kernel, name='filter_and_gram', out_shape=[jax.Shap...  52.6 us
    pallas_call x1, Pallas kernels, on_device(): pl.pallas_call(solve_kernel, name='solve', out_shape=[jax.ShapeDtypeStruc...  2.69 us

profile of v4, /device:TPU:1, one launch (start us, length us, event | category | flops | bytes accessed | tf_op | source)
XLA Modules:
  0.0 55.9 jit_solution(2224952250645075021)
XLA Ops:
  0.6 52.6 %filter_and_gram.1 = (f32[2,16,16,8,128]{4,3,2,1,0:T(8,128)S(1)}, f32[2,128]{1,0:T(2,128)S(1)}) custom-call(f32[16,256,128]{2,1,0:T(8,128)} %bitcast.2, f32[16,16,128]{2,1,0:T(8,128)} %pot_hbm.1, bf16[512,128]{1,0:T(8,128)(2,1)} %constant.2.clone.w_hbm), custom_call_target="tpu_custom_call" | custom-call | flops 1000000000 | bytes 5242880 | tf_op jit(solution)/shard_map/filter_and_gram/pallas_call | solution.py:454
  53.2 2.7 %solve.1 = (f32[16,256,128]{2,1,0:T(8,128)}, f32[16,16]{1,0:T(8,128)}) custom-call(f32[2,16,16,8,128]{4,3,2,1,0:T(8,128)S(1)} %get-tuple-element.6.filt, f32[2,128]{1,0:T(2,128)S(1)} %get-tuple-element.7.gram_ref), custom_call_target="tpu_custom_call" | custom-call | flops 100000000 | bytes 4194304 | tf_op jit(solution)/shard_map/solve/pallas_call | solution.py:497

commit v5 on v4

--- a/solution.py
+++ b/solution.py
@@ -367,7 +367,7 @@
     pltpu.make_async_copy(others, others, gsend.at[1]).wait()
 
 
-def solve_kernel(filt, gram_ref, out_hbm, factor_ref, out, out_sem):
+def solve_kernel(filt, gram_ref, out_hbm, factor_hbm, out, factor_ref, out_sem, factor_sem):
     def entry(i, j):
         at = NORB * (i % SUB) + j
         return jnp.broadcast_to(gram_ref[i // SUB : i // SUB + 1, at : at + 1], (SUB, LX))
@@ -411,6 +411,9 @@
 
     high, low = split(stack(inverse)[:, :NORB])
     lhs = jnp.concatenate([high, high, low], axis=1)
+
+    factor_ref[...] = gather({(j, i): value for (i, j), value in lower.items()})[:, :NORB]
+    factor_copy = pltpu.make_async_copy(factor_ref, factor_hbm, factor_sem)
 
     def out_copy(c):
         part = pl.ds(c * STEP * LY, STEP * LY)
@@ -441,7 +444,9 @@
                         block, 0, 1
                     )
         out_copy(c).start()
-    factor_ref[...] = gather({(j, i): value for (i, j), value in lower.items()})[:, :NORB]
+        if c == 0:
+            factor_copy.start()
+    factor_copy.wait()
     for c in range(LZ // STEP):
         out_copy(c).wait()
 
@@ -502,10 +507,12 @@
             jax.ShapeDtypeStruct((NORB, NORB), F32),
         ],
         in_specs=[vmem, vmem],
-        out_specs=[hbm, vmem],
+        out_specs=[hbm, hbm],
         scratch_shapes=[
             pltpu.VMEM((NORB, ROWS, LX), F32),
+            pltpu.VMEM((NORB, NORB), F32),
             dma((LZ // STEP,)),
+            dma(()),
         ],
         compiler_params=pltpu.CompilerParams(vmem_limit_bytes=24 * 2**20),
         cost_estimate=pl.CostEstimate(

time: 56 us -> 55.4 us (0.989)
  Pallas kernels: 55.3 us -> 54.7 us
    pallas_call x1, Pallas kernels: 2.69 us -> 2.11 us  [on_device(): pl.pallas_call(solve_kernel, name='solve', out_shape=[jax.ShapeDtypeStruc...]
where the time goes in v5:
time: 55.4 us; the launch traced here: 55.3 us
  Pallas kernels  54.7 us (99%)
  between operations  0.64 us (1%)
    pallas_call x1, Pallas kernels, on_device(): pl.pallas_call(filter_kernel, name='filter_and_gram', out_shape=[jax.Shap...  52.6 us
    pallas_call x1, Pallas kernels, on_device(): pl.pallas_call(solve_kernel, name='solve', out_shape=[jax.ShapeDtypeStruc...  2.11 us

profile of v5, /device:TPU:1, one launch (start us, length us, event | category | flops | bytes accessed | tf_op | source)
XLA Modules:
  0.0 55.3 jit_solution(7953909573383990034)
XLA Ops:
  0.6 52.6 %filter_and_gram.1 = (f32[2,16,16,8,128]{4,3,2,1,0:T(8,128)S(1)}, f32[2,128]{1,0:T(2,128)S(1)}) custom-call(f32[16,256,128]{2,1,0:T(8,128)} %bitcast.2, f32[16,16,128]{2,1,0:T(8,128)} %pot_hbm.1, bf16[512,128]{1,0:T(8,128)(2,1)} %constant.2.clone.w_hbm), custom_call_target="tpu_custom_call" | custom-call | flops 1000000000 | bytes 5242880 | tf_op jit(solution)/shard_map/filter_and_gram/pallas_call | solution.py:459
  53.2 2.1 %solve.1 = (f32[16,256,128]{2,1,0:T(8,128)}, f32[16,16]{1,0:T(8,128)}) custom-call(f32[2,16,16,8,128]{4,3,2,1,0:T(8,128)S(1)} %get-tuple-element.6.filt, f32[2,128]{1,0:T(2,128)S(1)} %get-tuple-element.7.gram_ref), custom_call_target="tpu_custom_call" | custom-call | flops 100000000 | bytes 4194304 | tf_op jit(solution)/shard_map/solve/pallas_call | solution.py:502

commit v6 on v5

--- a/solution.py
+++ b/solution.py
@@ -179,7 +179,7 @@
         copy.wait()
     pv[...] = pv[...] * F32(0.1) + F32(3.0 * TAPS[0] - 2.3)
 
-    def stencil(level, g, z):
+    def stencil(level, g, z, y_halo=True):
         buf = bufs[level]
         edges = jnp.where(
             lax.rem(lane, 2 * HALO) < HALO, from_left[level, g, z], from_right[level, g, z]
@@ -207,15 +207,23 @@
         for y in range(LY):
             total = pv[z, pl.ds(y, 1), :] * centre[y] + along_x[y * SUB : (y + 1) * SUB]
             for k in range(1, HALO + 1):
-                around = (
-                    buf[g, HALO + z + k, HALO + y] + buf[g, HALO + z - k, HALO + y]
-                ) + (buf[g, HALO + z, HALO + y + k] + buf[g, HALO + z, HALO + y - k])
+                around = buf[g, HALO + z + k, HALO + y] + buf[g, HALO + z - k, HALO + y]
+                rows_k = [r for r in (y + k, y - k) if y_halo or 0 <= r < LY]
+                if rows_k:
+                    beside = buf[g, HALO + z, HALO + rows_k[0]]
+                    for r in rows_k[1:]:
+                        beside = beside + buf[g, HALO + z, HALO + r]
+                    around = around + beside
                 total = total + F32(TAPS[k]) * around
             out.append(total)
         return out
 
-    def wait_halos(level, g, c):
-        for copy in y_copies(level, g, c) + x_copies(level, g, c):
+    def wait_y(level, g, c):
+        for copy in y_copies(level, g, c):
+            copy.wait_recv()
+
+    def wait_xz(level, g, c):
+        for copy in x_copies(level, g, c):
             copy.wait_recv()
 
         @pl.when(c == 0)
@@ -251,7 +259,8 @@
         @pl.loop(0, UNITS)
         def _(u, level=level):
             g, c = u // CHUNKS, lax.rem(u, CHUNKS)
-            wait_halos(level - 1, g, c)
+            wait_y(level - 1, g, c)
+            wait_xz(level - 1, g, c)
 
             if level == 2:
 
@@ -278,42 +287,57 @@
     tell(2)
     part[...] = jnp.zeros_like(part)
 
+    def add_gram(g, zs, ys):
+        @pl.when(g == GROUPS - 1)
+        def _():
+            total = jnp.zeros((2 * NORB, 2 * NORB), F32)
+            for z in zs:
+                wide = jnp.concatenate(
+                    [
+                        jnp.concatenate([last[k, z, y] for k in range(GROUPS)], axis=0)
+                        for y in ys
+                    ],
+                    axis=1,
+                )
+                both = jnp.concatenate(split(wide), axis=0)
+                total += lax.dot_general(
+                    both, both, (((1,), (1,)), ((), ())), preferred_element_type=F32
+                )
+            four = total[:NORB] + total[NORB:]
+            part[:, :NORB] += four[:, :NORB] + four[:, NORB:]
+
     @pl.loop(0, UNITS)
     def _(u):
         g, c = u // CHUNKS, lax.rem(u, CHUNKS)
-        wait_halos(2, g, c)
+        wait_xz(2, g, c)
 
         @pl.when(u == CHUNKS)
         def _():
             hear(2)
             tell(3)
 
-        @pl.loop(0, SLABS, unroll=UNROLL)
-        def _(s):
-            z = c * SLABS + s
-            new = stencil(2, g, z)
+        zs = [c * SLABS + s for s in range(SLABS)]
+        for z in zs:
+            new = stencil(2, g, z, y_halo=False)
             for y in range(LY):
                 last[g, z, y] = new[y] - buf1[g, HALO + z, HALO + y]
-
-        @pl.when(g == GROUPS - 1)
-        def _():
-            @pl.loop(0, SLABS, unroll=UNROLL)
-            def _(s):
-                z = c * SLABS + s
-                wide = jnp.concatenate(
-                    [
-                        jnp.concatenate([last[k, z, y] for k in range(GROUPS)], axis=0)
-                        for y in range(LY)
-                    ],
-                    axis=1,
-                )
-                high, low = split(wide)
-                both = jnp.concatenate([high, low], axis=0)
-                quad = lax.dot_general(
-                    both, both, (((1,), (1,)), ((), ())), preferred_element_type=F32
-                )
-                four = quad[:NORB] + quad[NORB:]
-                part[:, :NORB] += four[:, :NORB] + four[:, NORB:]
+        add_gram(g, zs, range(HALO, LY - HALO))
+
+    @pl.loop(0, UNITS)
+    def _(u):
+        g, c = u // CHUNKS, lax.rem(u, CHUNKS)
+        zs = [c * SLABS + s for s in range(SLABS)]
+        wait_y(2, g, c)
+        edge = [*range(HALO), *range(LY - HALO, LY)]
+        for z in zs:
+            for y in edge:
+                total = last[g, z, y]
+                for k in range(1, HALO + 1):
+                    for r in (y + k, y - k):
+                        if not 0 <= r < LY:
+                            total = total + F32(TAPS[k]) * buf2[g, HALO + z, HALO + r]
+                last[g, z, y] = total
+        add_gram(g, zs, edge)
 
     def wait_sends():
         @pl.loop(0, UNITS)

time: 55.4 us -> 54.8 us (0.989)
  Pallas kernels: 54.7 us -> 54 us
    pallas_call x1, Pallas kernels: 52.6 us -> 51.9 us  [on_device(): pl.pallas_call(filter_kernel, name='filter_and_gram', out_shape=[jax.Shap...]
where the time goes in v6:
time: 54.8 us; the launch traced here: 54.7 us
  Pallas kernels  54 us (99%)
  between operations  0.64 us (1%)
    pallas_call x1, Pallas kernels, on_device(): pl.pallas_call(filter_kernel, name='filter_and_gram', out_shape=[jax.Shap...  51.9 us
    pallas_call x1, Pallas kernels, on_device(): pl.pallas_call(solve_kernel, name='solve', out_shape=[jax.ShapeDtypeStruc...  2.11 us

profile of v6, /device:TPU:1, one launch (start us, length us, event | category | flops | bytes accessed | tf_op | source)
XLA Modules:
  0.0 54.7 jit_solution(7579175013899029381)
XLA Ops:
  0.6 51.9 %filter_and_gram.1 = (f32[2,16,16,8,128]{4,3,2,1,0:T(8,128)S(1)}, f32[2,128]{1,0:T(2,128)S(1)}) custom-call(f32[16,256,128]{2,1,0:T(8,128)} %bitcast.2, f32[16,16,128]{2,1,0:T(8,128)} %pot_hbm.1, bf16[512,128]{1,0:T(8,128)(2,1)} %constant.2.clone.w_hbm), custom_call_target="tpu_custom_call" | custom-call | flops 1000000000 | bytes 5242880 | tf_op jit(solution)/shard_map/filter_and_gram/pallas_call | solution.py:483
  52.6 2.1 %solve.1 = (f32[16,256,128]{2,1,0:T(8,128)}, f32[16,16]{1,0:T(8,128)}) custom-call(f32[2,16,16,8,128]{4,3,2,1,0:T(8,128)S(1)} %get-tuple-element.6.filt, f32[2,128]{1,0:T(2,128)S(1)} %get-tuple-element.7.gram_ref), custom_call_target="tpu_custom_call" | custom-call | flops 100000000 | bytes 4194304 | tf_op jit(solution)/shard_map/solve/pallas_call | solution.py:526

commit v7 on v6

--- a/solution.py
+++ b/solution.py
@@ -51,7 +51,7 @@
 
 def filter_kernel(
     orb_hbm, pot_hbm, w_hbm, last, gram_ref,
-    load, buf0, buf1, buf2, pack0, pack1, pack2, from_left, from_right, pv, w_ref, part, pair, seen, word,
+    load, buf0, buf1, buf2, pack0, pack1, pack2, from_left, from_right, pv, w_ref, part, seen, word,
     load_sem, small_sem, ysend, yrecv, xsend, xrecv, zsend, zrecv, gsend, grecv,
 ):
     bufs, packs = (buf0, buf1, buf2), (pack0, pack1, pack2)
@@ -234,8 +234,6 @@
         def _():
             z_copy(level, g, False).wait_recv()
 
-    core = lax.rem(here["gz"], 2)
-    layers = sizes["gz"] // 2
     rounds = (
         [("gx", d) for d in range(1, sizes["gx"])],
         [("gy", d) for d in range(1, sizes["gy"])],
@@ -354,41 +352,36 @@
 
     hear(3)
     moved = pltpu.roll(part[...] * F32(1.0 / CELLS), 0, 1, stride=NORB, stride_axis=0)
-    pair[0] = jnp.sum(moved.reshape(2, SUB, LX), axis=1)
-    to_core = remote(pair.at[0], pair.at[1], gsend.at[0], grecv.at[0], "gz", 1 - 2 * core)
-    to_core.start()
-    wait_sends()
-    to_core.wait_recv()
-    mine = (here["gx"] * sizes["gy"] + here["gy"]) * layers + here["gz"] // 2
-    seen[mine] = pair[0] + pair[1]
+    mine = (here["gx"] * sizes["gy"] + here["gy"]) * sizes["gz"] + here["gz"]
+    seen[mine] = jnp.sum(moved.reshape(2, SUB, LX), axis=1)
     offsets = [
         (dx, dy, dz)
         for dx in range(sizes["gx"])
         for dy in range(sizes["gy"])
-        for dz in range(layers)
+        for dz in range(sizes["gz"])
     ][1:]
-    ring = {"gx": sizes["gx"], "gy": sizes["gy"], "gz": layers}
 
     def hops(offset):
-        return sum(min(d, n - d) for d, n in zip(offset, ring.values()))
-
-    along = {axis: [at(axis, d * (2 if axis == "gz" else 1)) for d in range(ring[axis])] for axis in AXES}
+        dx, dy, dz = (min(d, sizes[axis] - d) for d, axis in zip(offset, AXES))
+        return 2 * (dx + dy) + dz
+
+    along = {axis: [at(axis, d)[axis] for d in range(sizes[axis])] for axis in AXES}
     for offset in sorted(offsets, key=hops, reverse=True):
         pltpu.make_async_remote_copy(
-            src_ref=seen.at[mine], dst_ref=seen.at[mine], send_sem=gsend.at[1],
-            recv_sem=grecv.at[1],
+            src_ref=seen.at[mine], dst_ref=seen.at[mine], send_sem=gsend.at[0],
+            recv_sem=grecv.at[0],
             device_id={axis: along[axis][d] for axis, d in zip(AXES, offset)},
             device_id_type=MESH,
         ).start()
+    wait_sends()
     others = seen.at[pl.ds(0, len(offsets))]
-    pltpu.make_async_copy(others, others, grecv.at[1]).wait()
+    pltpu.make_async_copy(others, others, grecv.at[0]).wait()
     terms = [seen[k] for k in range(len(offsets) + 1)]
     while len(terms) > 1:
         terms = [a + b for a, b in zip(terms[::2], terms[1::2])]
     value = terms[0]
     gram_ref[...] = value
-    to_core.wait_send()
-    pltpu.make_async_copy(others, others, gsend.at[1]).wait()
+    pltpu.make_async_copy(others, others, gsend.at[0]).wait()
 
 
 def solve_kernel(filt, gram_ref, out_hbm, factor_hbm, out, factor_ref, out_sem, factor_sem):
@@ -497,8 +490,7 @@
             pltpu.VMEM((LZ, LY, LX), F32),
             pltpu.VMEM((4 * LX, LX), BF16),
             pltpu.VMEM((NORB, LX), F32),
-            pltpu.VMEM((2, 2, LX), F32),
-            pltpu.VMEM((sizes["gx"] * sizes["gy"] * sizes["gz"] // 2, 2, LX), F32),
+            pltpu.VMEM((sizes["gx"] * sizes["gy"] * sizes["gz"], 2, LX), F32),
             pltpu.SemaphoreType.REGULAR((4,)),
             dma((UNITS,)),
             dma((2,)),
@@ -508,8 +500,8 @@
             dma((3, UNITS, 2)),
             dma((3, GROUPS, 2)),
             dma((3, GROUPS, 2)),
-            dma((2,)),
-            dma((2,)),
+            dma((1,)),
+            dma((1,)),
         ],
         compiler_params=pltpu.CompilerParams(
             collective_id=0, has_side_effects=True, vmem_limit_bytes=40 * 2**20

time: 54.8 us -> 54.5 us (level)
  no operation moved by 1% of the time
where the time goes in v7:
time: 54.5 us; the launch traced here: 54.4 us
  Pallas kernels  53.7 us (99%)
  between operations  0.64 us (1%)
    pallas_call x1, Pallas kernels, on_device(): pl.pallas_call(filter_kernel, name='filter_and_gram', out_shape=[jax.Shap...  51.6 us
    pallas_call x1, Pallas kernels, on_device(): pl.pallas_call(solve_kernel, name='solve', out_shape=[jax.ShapeDtypeStruc...  2.12 us

profile of v7, /device:TPU:1, one launch (start us, length us, event | category | flops | bytes accessed | tf_op | source)
XLA Modules:
  0.0 54.4 jit_solution(11072097249988760304)
XLA Ops:
  0.6 51.6 %filter_and_gram.1 = (f32[2,16,16,8,128]{4,3,2,1,0:T(8,128)S(1)}, f32[2,128]{1,0:T(2,128)S(1)}) custom-call(f32[16,256,128]{2,1,0:T(8,128)} %bitcast.2, f32[16,16,128]{2,1,0:T(8,128)} %pot_hbm.1, bf16[512,128]{1,0:T(8,128)(2,1)} %constant.2.clone.w_hbm), custom_call_target="tpu_custom_call" | custom-call | flops 1000000000 | bytes 5242880 | tf_op jit(solution)/shard_map/filter_and_gram/pallas_call | solution.py:476
  52.3 2.1 %solve.1 = (f32[16,256,128]{2,1,0:T(8,128)}, f32[16,16]{1,0:T(8,128)}) custom-call(f32[2,16,16,8,128]{4,3,2,1,0:T(8,128)S(1)} %get-tuple-element.6.filt, f32[2,128]{1,0:T(2,128)S(1)} %get-tuple-element.7.gram_ref), custom_call_target="tpu_custom_call" | custom-call | flops 100000000 | bytes 4194304 | tf_op jit(solution)/shard_map/solve/pallas_call | solution.py:518

commit v8 on v7

--- a/solution.py
+++ b/solution.py
@@ -24,6 +24,7 @@
 UNROLL = 4
 STEP = 2
 ROWS = LZ * LY
+PITCH = ROWS + SUB
 CELLS = 4194304
 F32, BF16 = jnp.float32, jnp.bfloat16
 MESH = pl.DeviceIdType.MESH
@@ -150,7 +151,7 @@
             packed = jnp.where(mine, moved, packed)
         return packed
 
-    flat = load.reshape(NORB * ROWS, LX)
+    flat = load.reshape((NORB + 1) * PITCH, LX)
 
     def start_unit(g, c):
         load_copy(g, c).wait()
@@ -160,7 +161,7 @@
             z = c * SLABS + s
             values = []
             for y in range(LY):
-                v = flat[pl.ds(g * SUB * ROWS + z * LY + y, SUB, stride=ROWS), :]
+                v = flat[pl.ds(g * SUB * PITCH + z * LY + y, SUB, stride=PITCH), :]
                 buf0[g, HALO + z, HALO + y] = v
                 values.append(v)
             pack0[g, z] = pack_edges(values)
@@ -483,7 +484,7 @@
         in_specs=[hbm] * 3,
         out_specs=[vmem, vmem],
         scratch_shapes=[
-            pltpu.VMEM((NORB, ROWS, LX), F32),
+            pltpu.VMEM((NORB + 1, PITCH, LX), F32),
             *[pltpu.VMEM((GROUPS, LZ + 2 * HALO, LY + 2 * HALO, SUB, LX), F32)] * 3,
             *[pltpu.VMEM((GROUPS, LZ, SUB, LX), F32)] * 3,
             *[pltpu.VMEM((3, GROUPS, LZ, SUB, LX), F32)] * 2,

time: 54.5 us -> 54.5 us (level)
  no operation moved by 1% of the time
where the time goes in v8:
time: 54.5 us; the launch traced here: 54.4 us
  Pallas kernels  53.7 us (99%)
  between operations  0.64 us (1%)
    pallas_call x1, Pallas kernels, on_device(): pl.pallas_call(filter_kernel, name='filter_and_gram', out_shape=[jax.Shap...  51.6 us
    pallas_call x1, Pallas kernels, on_device(): pl.pallas_call(solve_kernel, name='solve', out_shape=[jax.ShapeDtypeStruc...  2.11 us

profile of v8, /device:TPU:1, one launch (start us, length us, event | category | flops | bytes accessed | tf_op | source)
XLA Modules:
  0.0 54.4 jit_solution(5854356602533937513)
XLA Ops:
  0.6 51.6 %filter_and_gram.1 = (f32[2,16,16,8,128]{4,3,2,1,0:T(8,128)S(1)}, f32[2,128]{1,0:T(2,128)S(1)}) custom-call(f32[16,256,128]{2,1,0:T(8,128)} %bitcast.2, f32[16,16,128]{2,1,0:T(8,128)} %pot_hbm.1, bf16[512,128]{1,0:T(8,128)(2,1)} %constant.2.clone.w_hbm), custom_call_target="tpu_custom_call" | custom-call | flops 1000000000 | bytes 5242880 | tf_op jit(solution)/shard_map/filter_and_gram/pallas_call | solution.py:477
  52.3 2.1 %solve.1 = (f32[16,256,128]{2,1,0:T(8,128)}, f32[16,16]{1,0:T(8,128)}) custom-call(f32[2,16,16,8,128]{4,3,2,1,0:T(8,128)S(1)} %get-tuple-element.6.filt, f32[2,128]{1,0:T(2,128)S(1)} %get-tuple-element.7.gram_ref), custom_call_target="tpu_custom_call" | custom-call | flops 100000000 | bytes 4194304 | tf_op jit(solution)/shard_map/solve/pallas_call | solution.py:519

commit v9 on v7

--- a/solution.py
+++ b/solution.py
@@ -460,7 +460,7 @@
                     out[pl.ds(g * SUB, SUB), pl.ds(z * LY + start, SUB), :] = jnp.swapaxes(
                         block, 0, 1
                     )
-        out_copy(c).start()
+        out_copy(c).start(priority=c % 2)
         if c == 0:
             factor_copy.start()
     factor_copy.wait()

time: 54.5 us -> 54.5 us (level)
  no operation moved by 1% of the time
where the time goes in v9:
time: 54.5 us; the launch traced here: 54.4 us
  Pallas kernels  53.7 us (99%)
  between operations  0.64 us (1%)
    pallas_call x1, Pallas kernels, on_device(): pl.pallas_call(filter_kernel, name='filter_and_gram', out_shape=[jax.Shap...  51.6 us
    pallas_call x1, Pallas kernels, on_device(): pl.pallas_call(solve_kernel, name='solve', out_shape=[jax.ShapeDtypeStruc...  2.12 us

profile of v9, /device:TPU:1, one launch (start us, length us, event | category | flops | bytes accessed | tf_op | source)
XLA Modules:
  0.0 54.4 jit_solution(16995259027992408316)
XLA Ops:
  0.6 51.6 %filter_and_gram.1 = (f32[2,16,16,8,128]{4,3,2,1,0:T(8,128)S(1)}, f32[2,128]{1,0:T(2,128)S(1)}) custom-call(f32[16,256,128]{2,1,0:T(8,128)} %bitcast.2, f32[16,16,128]{2,1,0:T(8,128)} %pot_hbm.1, bf16[512,128]{1,0:T(8,128)(2,1)} %constant.2.clone.w_hbm), custom_call_target="tpu_custom_call" | custom-call | flops 1000000000 | bytes 5242880 | tf_op jit(solution)/shard_map/filter_and_gram/pallas_call | solution.py:476
  52.3 2.1 %solve.1 = (f32[16,256,128]{2,1,0:T(8,128)}, f32[16,16]{1,0:T(8,128)}) custom-call(f32[2,16,16,8,128]{4,3,2,1,0:T(8,128)S(1)} %get-tuple-element.6.filt, f32[2,128]{1,0:T(2,128)S(1)} %get-tuple-element.7.gram_ref), custom_call_target="tpu_custom_call" | custom-call | flops 100000000 | bytes 4194304 | tf_op jit(solution)/shard_map/solve/pallas_call | solution.py:518
